TPU v7x, 32 devices: a whole 2x2x4 slice. The times are simulated.
32 devices in a mesh: groups: 2 (over y), tile: 16 (over z, x, core).
Axes of the slice: x: 2, y: 2, z: 4, core: 2. Of those that a mesh axis runs over, the one named last changes fastest.
Arguments:
- exposure_pixels: bfloat16 [4096, 64, 128], P(('groups', 'tile')), parts along dimension 0, may hold values from -6 to 6
- block_band: int32 [4096], P(('groups', 'tile')), parts along dimension 0, may hold values from 0 to 5
- block_tile: int32 [4096], P(('groups', 'tile')), parts along dimension 0, may hold values from 0 to 15, as said below
- block_row: int32 [4096], P(('groups', 'tile')), parts along dimension 0, may hold values from 0 to 15
- band_weights: bfloat16 [6, 102, 64], replicated, may hold values from -0.75 to 0.75
- psf_kernel: float32 [102, 25], replicated, may hold values from -1 to 1
- gal_tile: int32 [2048], P(('groups', 'tile')), parts along dimension 0, may hold values from 0 to 15, as said below
- gal_row: int32 [2048], P(('groups', 'tile')), parts along dimension 0, may hold values from 0 to 15
- gal_col: int32 [2048], P(('groups', 'tile')), parts along dimension 0, may hold values from 0 to 127
- gal_shift: int32 [2048], P(('groups', 'tile')), parts along dimension 0, may hold values from 0 to 38
Outputs:
- matched_cube: bfloat16 [512, 102, 128], P(('groups', 'tile')), parts along dimension 0
- rest_spectra: bfloat16 [2048, 64], P(('groups', 'tile')), parts along dimension 0
There are 2 independent parts, one for each index of `groups`. A program takes and returns all parts, laid end to end along the dimension named above; an argument that names none is the same for every part. Nothing has to cross between parts.
Inputs may be any that keep to these rules, and one draw needn't show every extreme that they name: `block_tile`: among the 128 blocks of one device at most 16 fall on any one tile; in every draw every device sends exactly 16 blocks to some tile. `gal_tile`: among the 64 catalog entries of one device at most 8 fall on any one tile; in every draw every device has exactly 8 entries on some tile.
All inputs are finite; a program needn't handle non-finite values.
Results may differ from a plain program's by a relative error of at most 0.0054.
Values may be sent and summed in bfloat16 or wider, within the bound.
A program may use at most 128 MiB of HBM per device.

v0:
```python
import jax
import jax.numpy as jnp
from jax import lax
from jax.sharding import PartitionSpec as P

KW = 5
NW = 64
TROWS = 16


def with_halo(cells, sides, width):
    for axis, dim in sides:
        count = lax.axis_size(axis)
        ends = count - 1
        head = lax.slice_in_dim(cells, 0, width, axis=dim)
        tail = lax.slice_in_dim(cells, cells.shape[dim] - width, cells.shape[dim], axis=dim)
        cells = jnp.concatenate(
            [
                lax.ppermute(tail, axis, [(i, (i + 1) % count) for i in range(ends)]),
                cells,
                lax.ppermute(head, axis, [((i + 1) % count, i) for i in range(ends)]),
            ],
            axis=dim,
        )
    return cells


def resample(band_onehot, band_weights, samples):
    selected = jnp.einsum(
        "bk,kcs->bcs", band_onehot, band_weights, preferred_element_type=jnp.float32
    ).astype(jnp.bfloat16)
    return jnp.einsum("bcs,bsp->bcp", selected, samples, preferred_element_type=jnp.float32).astype(
        jnp.bfloat16
    )


def rank_before(tiles):
    length = tiles.shape[-1]
    positions = jnp.arange(length, dtype=jnp.int32)
    earlier = (tiles[..., :, None] == tiles[..., None, :]) & (
        positions[None, :] < positions[:, None]
    )
    return jnp.sum(earlier.astype(jnp.int32), axis=-1)


def shift_columns(field, offset):
    if offset == 0:
        return field
    width = field.shape[2]
    filler = jnp.zeros((field.shape[0], field.shape[1], abs(offset)), field.dtype)
    if offset > 0:
        return jnp.concatenate([field[:, :, offset:], filler], axis=2)
    return jnp.concatenate([filler, field[:, :, : width + offset]], axis=2)


def body(
    exposure_pixels,
    block_band,
    block_tile,
    block_row,
    band_weights,
    psf_kernel,
    gal_tile,
    gal_row,
    gal_col,
    gal_shift,
):
    tile_count = lax.axis_size("tile")
    blocks_here = exposure_pixels.shape[0]
    capacity = 2 * blocks_here // tile_count
    slot_count = tile_count * capacity
    channels = band_weights.shape[1]
    columns = exposure_pixels.shape[2]
    band_total = band_weights.shape[0]
    gal_here = gal_tile.shape[0]
    rank_in = rank_before(block_tile)
    slot_index = block_tile * capacity + rank_in
    info_rows = jnp.full((slot_count,), -1, jnp.int32).at[slot_index].set(block_row)
    info_bands = jnp.zeros((slot_count,), jnp.int32).at[slot_index].set(block_band)
    slot_info = jnp.stack([info_rows, info_bands], axis=1)
    band_range = jnp.arange(band_total, dtype=jnp.int32)
    band_onehot = (block_band[:, None] == band_range[None, :]).astype(jnp.bfloat16)
    spectra = resample(band_onehot, band_weights, exposure_pixels)
    outgoing = jnp.zeros((slot_count, channels, columns), jnp.bfloat16).at[slot_index].set(spectra)
    arrived, arrived_info = (
        lax.all_to_all(outgoing, "tile", split_axis=0, concat_axis=0, tiled=True),
        lax.all_to_all(slot_info, "tile", split_axis=0, concat_axis=0, tiled=True),
    )
    row_range = jnp.arange(TROWS, dtype=jnp.int32)
    row_table = (arrived_info[:, 0][None, :] == row_range[:, None]).astype(jnp.bfloat16)
    row_sums = jnp.dot(
        row_table,
        arrived.reshape(slot_count, channels * columns),
        preferred_element_type=jnp.float32,
    )
    counts = jnp.sum(row_table.astype(jnp.float32), axis=1)
    coadded = (
        (row_sums / jnp.maximum(counts, 1.0)[:, None])
        .reshape(TROWS, channels, columns)
        .astype(jnp.bfloat16)
    )
    radius = KW // 2
    padded = with_halo(coadded, (("tile", 0),), radius)
    shifted_fields = [shift_columns(padded, offset_col - radius) for offset_col in range(KW)]
    terms = []
    for offset_row in range(KW):
        for offset_col in range(KW):
            tap_weight = psf_kernel[:, offset_row * KW + offset_col][None, :, None]
            window_cells = shifted_fields[offset_col][offset_row : offset_row + TROWS]
            terms.append(tap_weight * window_cells.astype(jnp.float32))
    matched_sum = terms[0]
    for extra in terms[1:]:
        matched_sum = matched_sum + extra
    matched_cube = matched_sum.astype(jnp.bfloat16)
    shift_span = channels - NW + 1
    packed_word = ((gal_tile * TROWS + gal_row) * columns + gal_col) * shift_span + gal_shift
    all_words = lax.all_gather(packed_word, "tile", axis=0, tiled=True)
    cat_shift = all_words % shift_span
    rest_word = all_words // shift_span
    cat_col = rest_word % columns
    strip_word = rest_word // columns
    cat_row = strip_word % TROWS
    cat_tile = strip_word // TROWS
    owned = cat_tile == lax.axis_index("tile")
    slot_depth = min(8, gal_here)
    slot_total = tile_count * slot_depth
    all_rank = rank_before(cat_tile.reshape(tile_count, gal_here)).reshape(-1)
    holder = jnp.arange(tile_count * gal_here, dtype=jnp.int32) // gal_here
    slot_place = jnp.where(owned, holder * slot_depth + all_rank, slot_total)
    slot_row = jnp.zeros((slot_total,), jnp.int32).at[slot_place].set(cat_row, mode="drop")
    slot_col = jnp.zeros((slot_total,), jnp.int32).at[slot_place].set(cat_col, mode="drop")
    slot_shift = jnp.zeros((slot_total,), jnp.int32).at[slot_place].set(cat_shift, mode="drop")
    row_onehot = (slot_row[:, None] == row_range[None, :]).astype(jnp.bfloat16)
    picked_rows = jnp.dot(
        row_onehot,
        matched_cube.reshape(TROWS, channels * columns),
        preferred_element_type=jnp.float32,
    ).astype(jnp.bfloat16)
    picked_rows = picked_rows.reshape(slot_total, channels, columns)
    col_onehot = (slot_col[:, None] == jnp.arange(columns, dtype=jnp.int32)[None, :]).astype(
        jnp.bfloat16
    )
    spectra_at = jnp.einsum(
        "scp,sp->sc", picked_rows, col_onehot, preferred_element_type=jnp.float32
    )
    channel_window = slot_shift[:, None] + jnp.arange(NW, dtype=jnp.int32)[None, :]
    slot_values = jnp.take_along_axis(spectra_at, channel_window, axis=1).astype(jnp.bfloat16)
    window_values = slot_values[jnp.minimum(slot_place, slot_total - 1)]
    partial_value = jnp.where(owned[:, None], window_values.astype(jnp.float32), 0.0)
    rest_spectra = lax.psum_scatter(partial_value, "tile", scatter_dimension=0, tiled=True).astype(
        jnp.bfloat16
    )
    return (matched_cube, rest_spectra)


def solution(mesh):
    placed = (
        P(("groups", "tile"), None, None),
        P(("groups", "tile")),
        P(("groups", "tile")),
        P(("groups", "tile")),
        P(),
        P(),
        P(("groups", "tile")),
        P(("groups", "tile")),
        P(("groups", "tile")),
        P(("groups", "tile")),
    )
    return jax.shard_map(
        body,
        mesh=mesh,
        in_specs=placed,
        out_specs=(P(("groups", "tile"), None, None), P(("groups", "tile"), None)),
        check_vma=False,
    )
```

profile of v0, /device:TPU:0, one launch (start us, length us, event | category | flops | bytes accessed | tf_op | source)
XLA Modules:
  0.0 390.6 jit_solution(10483089102679510045)
XLA Ops:
  7.2 1.0 convert_reduce_fusion.1
  8.2 0.7 compare_select_fusion.4
  8.8 1.1 scatter_custom_fusion.1
  10.0 1.1 scatter_custom_fusion
  11.2 0.6 copy.38
  11.9 7.4 %all-to-all-start = ((s32[16,16,2]{1,2,0:T(2,128)}), s32[16,16,2]{1,2,0:T(2,128)S(1)}, u32[]{:S(2)}, u32[]{:S(2)}) async-start(s32[16,16,2]{1,2,0:T(2,128)} %copy.38), calls=%async_computation | async-start | bytes 32768 | tf_op jit(solution)/shard_map/all_to_all | solution.py:87
  19.2 2.9 convolution_convert_fusion.2
  22.1 4.0 %copy.41 = bf16[128,102,64]{1,2,0:T(8,128)(2,1)} copy(bf16[128,102,64]{0,1,2:T(8,128)(2,1)} %convolution_convert_fusion.2) | data formatting | bytes 3342336 | tf_op jit(solution)/shard_map/convert_element_type | solution.py:31
  26.1 5.3 %convolution_convert_fusion.1 = bf16[128,102,128]{2,1,0:T(8,128)(2,1)} fusion(bf16[128,102,64]{1,2,0:T(8,128)(2,1)} %copy.41, bf16[128,64,128]{2,1,0:T(8,128)(2,1)S(1)} %copy-done), kind=kOutput, calls=%fused_computation.11 | convolution fusion | flops 215580672 | bytes 7110656 | tf_op jit(solution)/shard_map/bcs,bsp->bcp/dot_general | solution.py:32
  31.4 3.7 broadcast_in_dim.28
  35.2 19.0 %scatter_fusion = bf16[256,102,128]{2,1,0:T(8,128)(2,1)} fusion(bf16[256,102,128]{2,1,0:T(8,128)(2,1)} %broadcast_in_dim.28, s32[128]{0:T(128)S(1)} %compare_select_fusion.4, bf16[128,102,128]{2,1,0:T(8,128)(2,1)} %convolution_convert_fusion.1), kind=kCustom, calls=%fused_computation.4 | custom fusion | bytes 10027520 | tf_op jit(solution)/shard_map/scatter | solution.py:84
  54.2 6.2 %all-to-all-start.1 = ((bf16[256,102,128]{2,1,0:T(8,128)(2,1)}), bf16[256,102,128]{2,1,0:T(8,128)(2,1)}, u32[]{:S(2)}, u32[]{:S(2)}) async-start(bf16[256,102,128]{2,1,0:T(8,128)(2,1)} %scatter_fusion), calls=%async_computation.1 | async-start | bytes 13631488 | tf_op jit(solution)/shard_map/all_to_all | solution.py:86
  61.8 148.9 %all-reduce.4 = s32[1024]{0:T(1024)S(1)} all-reduce(s32[1024]{0:T(1024)S(1)} %add_dynamic-update-slice_fusion), channel_id=1, replica_groups=mesh['groups'=2,'tile'=16] {'tile'}, use_global_device_ids=true, to_apply=%add.4 | all-reduce | flops 1024 | bytes 8192
  211.5 4.3 %scatter_custom_fusion.5 = s32[128]{0:T(128)S(1)} fusion(s32[1024]{0:T(1024)S(1)} %compare_select_fusion.3, s32[1024]{0:T(1024)S(1)} %get-tuple-element.55, s32[]{:T(128)} %constant.96.clone.1), kind=kCustom, calls=%fused_computation.124 | custom fusion | bytes 516 | tf_op jit(solution)/shard_map/scatter | solution.py:131
  215.8 4.3 %scatter_custom_fusion.3 = s32[128]{0:T(128)S(1)} fusion(s32[1024]{0:T(1024)S(1)} %compare_select_fusion.3, s32[1024]{0:T(1024)S(1)} %get-tuple-element.54, s32[]{:T(128)} %constant.96.clone.1), kind=kCustom, calls=%fused_computation.128 | custom fusion | bytes 516 | tf_op jit(solution)/shard_map/scatter | solution.py:132
  220.5 11.0 %copy.42 = bf16[256,102,128]{0,2,1:T(8,128)(2,1)} copy(bf16[256,102,128]{2,1,0:T(8,128)(2,1)} %all-to-all-done.1) | data formatting | bytes 13369344 | tf_op jit(solution)/shard_map/all_to_all | solution.py:86
  231.5 4.8 %fusion = bf16[16,13056]{1,0:T(8,128)(2,1)S(1)} fusion(bf16[256,13056]{0,1:T(8,128)(2,1)} %bitcast.74, f32[16]{0:T(128)S(1)} %broadcast_maximum_fusion, s32[256]{0:T(256)S(1)} %bitcast.78), kind=kOutput, calls=%fused_computation.10 | convolution fusion | flops 107376640 | bytes 7103552 | tf_op jit(solution)/shard_map/dot_general | solution.py:91
  236.5 1.5 collective-permute-start
  238.0 4.3 %scatter_custom_fusion.4 = s32[128]{0:T(128)S(1)} fusion(s32[1024]{0:T(1024)S(1)} %compare_select_fusion.3, s32[1024]{0:T(1024)S(1)} %get-tuple-element.56, s32[]{:T(128)} %constant.96.clone.1), kind=kCustom, calls=%fused_computation.126 | custom fusion | bytes 516 | tf_op jit(solution)/shard_map/scatter | solution.py:130
  242.7 1.3 collective-permute-start.1
  244.2 3.3 collective-permute-done.1
  248.0 4.5 %add_convert_fusion = bf16[16,102,128]{2,1,0:T(8,128)(2,1)S(1)} fusion(bf16[16,102,128]{2,1,0:T(8,128)(2,1)S(1)} %convert_element_type.123, bf16[18,102,128]{2,1,0:T(8,128)(2,1)S(1)} %get-tuple-element.26, bf16[18,102,128]{2,1,0:T(8,128)(2,1)S(1)} %get-tuple-element.22, f32[102]{0:T(128)S(1)} %get-tuple-element.52, f32[102]{0:T(128)S(1)} %get-tuple-element.53, ...), kind=kLoop, calls=%fused_computation.13 | loop fusion | flops 15667200 | bytes 4581432 | tf_op jit(solution)/shard_map/convert_element_type | solution.py:114
  252.4 2.8 convolution_convert_fusion
  255.2 5.7 %copy.43 = bf16[128,13056]{0,1:T(8,128)(2,1)} copy(bf16[128,13056]{1,0:T(8,128)(2,1)} %convolution_convert_fusion) | data formatting | bytes 6684672 | tf_op jit(solution)/shard_map/convert_element_type | solution.py:138
  260.9 5.7 %copy.45 = bf16[128,102,128]{2,1,0:T(8,128)(2,1)} copy(bf16[128,102,128]{0,2,1:T(8,128)(2,1)} %bitcast.75) | data formatting | bytes 6684672 | tf_op jit(solution)/shard_map/reshape | solution.py:139
  266.6 3.8 fusion.3
  270.4 50.1 %gather_fusion.1 = bf16[8192]{0:T(1024)(128)(2,1)S(1)} fusion(f32[128,102]{1,0:T(8,128)S(1)} %bitcast.73, s32[8192]{0:T(1024)S(1)} %reshape.145), kind=kCustom, calls=%fused_computation.1 | custom fusion | bytes 98304 | tf_op jit(solution)/shard_map/jit(take_along_axis)/gather | solution.py:147
  320.7 3.2 gather_fusion
  324.0 1.0 convert_select_fusion
  325.0 0.8 copy.44
  325.8 56.6 %reduce-scatter.2.cloned.1.call-done = f32[64,64]{1,0:T(8,128)} async-done(((f32[1024,64]{1,0:T(8,128)}), f32[64,64]{1,0:T(8,128)}) %reduce-scatter.2.cloned.1.call-update) | async-done | bytes 16400 | tf_op jit(solution)/shard_map/reduce_scatter | solution.py:150
  382.4 1.4 convert_element_type.154
  (54 shorter events, 3.6 us)
Async XLA Ops:
  7.2 19.0 %copy-start = (bf16[128,64,128]{2,1,0:T(8,128)(2,1)S(1)}, bf16[128,64,128]{2,1,0:T(8,128)(2,1)}, u32[]{:S(2)}) copy-start(bf16[128,64,128]{2,1,0:T(8,128)(2,1)} %param.10) | copy-start | bytes 6291460
  11.9 42.3 %all-to-all-start = ((s32[16,16,2]{1,2,0:T(2,128)}), s32[16,16,2]{1,2,0:T(2,128)S(1)}, u32[]{:S(2)}, u32[]{:S(2)}) async-start(s32[16,16,2]{1,2,0:T(2,128)} %copy.38), calls=%async_computation | async-start | bytes 32768 | tf_op jit(solution)/shard_map/all_to_all | solution.py:87
  54.1 6.3 %copy-start.6 = (u32[32]{0:T(128)S(1)}, u32[32]{0:T(128)}, u32[]{:S(2)}) copy-start(u32[32]{0:T(128)} %constant.138) | copy-start | bytes 388
  54.1 7.5 %copy-start.2 = (s32[64]{0:T(128)S(1)}, s32[64]{0:T(128)}, u32[]{:S(2)}) copy-start(s32[64]{0:T(128)} %param.19) | copy-start | bytes 772
  54.1 7.5 %copy-start.3 = (s32[64]{0:T(128)S(1)}, s32[64]{0:T(128)}, u32[]{:S(2)}) copy-start(s32[64]{0:T(128)} %param.18) | copy-start | bytes 772
  54.1 7.5 %copy-start.4 = (s32[64]{0:T(128)S(1)}, s32[64]{0:T(128)}, u32[]{:S(2)}) copy-start(s32[64]{0:T(128)} %param.17) | copy-start | bytes 772
  54.1 7.5 %copy-start.5 = (s32[64]{0:T(128)S(1)}, s32[64]{0:T(128)}, u32[]{:S(2)}) copy-start(s32[64]{0:T(128)} %param.16) | copy-start | bytes 772
  54.1 165.9 %copy-start.1 = (f32[102,25]{0,1:T(8,128)S(1)}, f32[102,25]{0,1:T(8,128)}, u32[]{:S(2)}) copy-start(f32[102,25]{0,1:T(8,128)} %param.15) | copy-start | bytes 30604
  54.2 166.4 %all-to-all-start.1 = ((bf16[256,102,128]{2,1,0:T(8,128)(2,1)}), bf16[256,102,128]{2,1,0:T(8,128)(2,1)}, u32[]{:S(2)}, u32[]{:S(2)}) async-start(bf16[256,102,128]{2,1,0:T(8,128)(2,1)} %scatter_fusion), calls=%async_computation.1 | async-start | bytes 13631488 | tf_op jit(solution)/shard_map/all_to_all | solution.py:86
  60.3 322.1 %reduce-scatter.2.cloned.1.call-start = ((), (), s32[]{:S(2)}) async-start(), calls=%async_computation.3 | async-start | bytes 557056 | tf_op jit(solution)/shard_map/reduce_scatter | solution.py:150
  236.5 7.5 %collective-permute-start = (bf16[2,102,128]{2,1,0:T(8,128)(2,1)S(1)}, bf16[2,102,128]{2,1,0:T(8,128)(2,1)S(1)}, u32[]{:S(2)}, u32[]{:S(2)}) collective-permute-start(bf16[2,102,128]{2,1,0:T(8,128)(2,1)S(1)} %slice.181), channel_id=1, source_target_pairs={{0,1},{1,2},{2,3},{3,4},{4,5},{5,6},{6,7},{7,8},{8,9},{9,10},{10,1... | collective-permute-start | bytes 156680 | tf_op jit(solution)/shard_map/ppermute | solution.py:19
  242.7 4.8 %collective-permute-start.1 = (bf16[2,102,128]{2,1,0:T(8,128)(2,1)S(1)}, bf16[2,102,128]{2,1,0:T(8,128)(2,1)S(1)}, u32[]{:S(2)}, u32[]{:S(2)}) collective-permute-start(bf16[2,102,128]{2,1,0:T(8,128)(2,1)S(1)} %slice.183), channel_id=1, source_target_pairs={{1,0},{2,1},{3,2},{4,3},{5,4},{6,5},{7,6},{8,7},{9,8},{10,9},{11,1... | collective-permute-start | bytes 156680 | tf_op jit(solution)/shard_map/ppermute | solution.py:21
Sparse Core Ops, SparseCore 0:
  325.1 57.2 reduce-scatter.1
where the time goes:
time: 392 us; the launch traced here: 391 us
  blocking collectives  149 us (38%)
  local copies, waits for them, and re-layouts  121 us (31%)
  waiting for transfers between devices  59.9 us (15%)
  matrix products  19.5 us (5%)
  starting transfers between devices  16.3 us (4%)
  between operations  15 us (4%)
  other arithmetic  9.58 us (2%)
    unnamed x1, blocking collectives  149 us
    reduce_scatter x1, waiting for transfers between devices, body(): lax.psum_scatter(partial_value, 'tile', scatter_dimension=0, tiled=True)  56.6 us
    gather x3, local copies, waits for them, and re-layouts, body(): jnp.take_along_axis(spectra_at, channel_window, axis=1).astype(jnp.bfloat16)  50.3 us
    scatter x1, local copies, waits for them, and re-layouts, body(): jnp.zeros((slot_count, channels, columns), jnp.bfloat16).at[slot_index]  19 us
    all_to_all x1, local copies, waits for them, and re-layouts, body(): lax.all_to_all(outgoing, 'tile', split_axis=0, concat_axis=0, tiled=True)  11 us
  transfers between devices with their start and end apart: 5, of which 2 were waited for; matrix products, arithmetic and copies ran while one was open for 13% of the time, Pallas kernels for 0%

commit v1 on v0

v1 whole, which is shorter than its diff:
```python
import functools

import jax
import jax.numpy as jnp
from jax import lax
from jax.experimental import pallas as pl
from jax.experimental.pallas import tpu as pltpu
from jax.sharding import PartitionSpec as P

KW = 5
NW = 64
TROWS = 16
F32 = jnp.float32
BF16 = jnp.bfloat16
CHUNKS = 2
GROUP = 8


def partial_sums_kernel(place_ref, band_ref, pixels_ref, weights_ref, *rest):
    outs, total = rest[:-1], rest[-1]
    blocks = pixels_ref.shape[0]
    rows_out = outs[0].shape[0]

    def clear(i, _):
        total[i] = jnp.zeros(total.shape[1:], F32)
        return 0

    lax.fori_loop(0, total.shape[0], clear, 0, unroll=4)

    def step(i, _):
        spectra = []
        for k in range(GROUP):
            b = i * GROUP + k
            spectra.append(
                jnp.dot(weights_ref[band_ref[b]], pixels_ref[b], preferred_element_type=F32)
            )
        for k in range(GROUP):
            b = i * GROUP + k
            total[place_ref[b]] += spectra[k].astype(BF16).astype(F32)
        return 0

    lax.fori_loop(0, blocks // GROUP, step, 0)

    for n, out in enumerate(outs):

        def emit(i, _, n=n, out=out):
            out[i] = total[n * rows_out + i].astype(BF16)
            return 0

        lax.fori_loop(0, rows_out, emit, 0, unroll=4)


def partial_sums(place, band, pixels, weights, rows, pieces):
    channels, columns = weights.shape[1], pixels.shape[2]
    smem = pl.BlockSpec(memory_space=pltpu.SMEM)
    vmem = pl.BlockSpec(memory_space=pltpu.VMEM)
    return pl.pallas_call(
        partial_sums_kernel,
        out_shape=[jax.ShapeDtypeStruct((rows // pieces, channels, columns), BF16)] * pieces,
        in_specs=[smem, smem, vmem, vmem],
        out_specs=[vmem] * pieces,
        scratch_shapes=[pltpu.VMEM((rows, channels, columns), F32)],
        compiler_params=pltpu.CompilerParams(vmem_limit_bytes=48 * 1024 * 1024),
        name="partial_sums",
    )(place, band, pixels, weights)


def tile_row_sums(pixels, band, tile, row, weights):
    me = lax.axis_index("tile")
    z, x, c = me // 4, (me // 2) % 2, me % 2
    dest_z, dest_x, dest_c = tile // 4, (tile // 2) % 2, tile % 2
    far_x, far_c = (dest_x + x) % 2, (dest_c + c) % 2
    part = TROWS // CHUNKS
    place = (((far_c * 2 + far_x) * CHUNKS + row // part) * 4 + dest_z) * part + row % part
    out = partial_sums(place, band, pixels, weights, 16 * TROWS, 4 * CHUNKS)
    other_core = [(i, i ^ 1) for i in range(16)]
    other_x = [(i, i ^ 2) for i in range(16)]
    keep = lambda far, chunk: out[far * CHUNKS + chunk]
    send = lambda far, chunk: out[(2 + far) * CHUNKS + chunk]
    arrived = {}
    for far in (1, 0):
        for chunk in range(CHUNKS):
            arrived[far, chunk] = lax.ppermute(send(far, chunk), "tile", other_core)
    wide = lambda a: a.astype(F32)
    crossed = []
    for chunk in range(CHUNKS):
        chip = (wide(keep(1, chunk)) + wide(arrived[1, chunk])).astype(BF16)
        crossed.append(lax.ppermute(chip, "tile", other_x))
    sums = []
    for chunk in range(CHUNKS):
        plane = (wide(keep(0, chunk)) + wide(arrived[0, chunk]) + wide(crossed[chunk])).astype(BF16)
        plane = plane.reshape((4, part) + plane.shape[1:])
        pick = lambda at: wide(lax.dynamic_index_in_dim(plane, jnp.clip(at, 0, 3), 0, keepdims=False))
        up = down = None
        for dist in (3, 2, 1):
            up_term, down_term = pick(z + dist), pick(z - dist)
            if up is not None:
                up_term, down_term = up_term + wide(up), down_term + wide(down)
            forward = [(i, i + 4) for i in range(4 * (4 - dist))]
            backward = [(15 - i, 15 - j) for i, j in forward]
            up = lax.ppermute(up_term.astype(BF16), "tile", forward)
            down = lax.ppermute(down_term.astype(BF16), "tile", backward)
        sums.append(pick(z) + wide(up) + wide(down))
    return jnp.concatenate(sums, axis=0)


def tile_row_sums_any(pixels, band, tile, row, weights):
    tile_count = lax.axis_size("tile")
    blocks = pixels.shape[0]
    capacity = 2 * blocks // tile_count
    slots = tile_count * capacity
    place = tile * capacity + rank_before(tile)
    tag = jnp.full((slots,), -1, jnp.int32).at[place].set(row * weights.shape[0] + band)
    packed = jnp.zeros((slots,) + pixels.shape[1:], BF16).at[place].set(pixels)
    packed = lax.all_to_all(packed, "tile", split_axis=0, concat_axis=0, tiled=True)
    tag = lax.all_to_all(tag, "tile", split_axis=0, concat_axis=0, tiled=True)
    bands = jnp.maximum(tag, 0) % weights.shape[0]
    rows = jnp.where(tag < 0, -1, tag // weights.shape[0])
    spectra = jnp.einsum("bcs,bsp->bcp", weights[bands], packed, preferred_element_type=F32)
    spectra = spectra.astype(BF16).reshape(slots, -1)
    table = (rows[None, :] == jnp.arange(TROWS)[:, None]).astype(BF16)
    sums = jnp.dot(table, spectra, preferred_element_type=F32)
    return sums.reshape(TROWS, weights.shape[1], pixels.shape[2])


def rank_before(tiles):
    positions = jnp.arange(tiles.shape[0], dtype=jnp.int32)
    earlier = (tiles[:, None] == tiles[None, :]) & (positions[None, :] < positions[:, None])
    return jnp.sum(earlier.astype(jnp.int32), axis=-1)


def with_halo(cells, width):
    count = lax.axis_size("tile")
    ends = count - 1
    above = lax.ppermute(cells[-width:], "tile", [(i, i + 1) for i in range(ends)])
    below = lax.ppermute(cells[:width], "tile", [(i + 1, i) for i in range(ends)])
    return jnp.concatenate([above, cells, below], axis=0)


def psf_match(coadded, psf_kernel):
    radius = KW // 2
    columns = coadded.shape[2]
    padded = jnp.pad(with_halo(coadded, radius), ((0, 0), (0, 0), (radius, radius)))
    total = None
    for dy in range(KW):
        for dx in range(KW):
            tap = psf_kernel[:, dy * KW + dx][None, :, None]
            term = tap * padded[dy : dy + TROWS, :, dx : dx + columns].astype(F32)
            total = term if total is None else total + term
    return total.astype(BF16)


def body(
    exposure_pixels,
    block_band,
    block_tile,
    block_row,
    band_weights,
    psf_kernel,
    gal_tile,
    gal_row,
    gal_col,
    gal_shift,
):
    tile_count = lax.axis_size("tile")
    channels, columns = band_weights.shape[1], exposure_pixels.shape[2]
    gal_here = gal_tile.shape[0]
    depth = min(8, gal_here)
    span = channels - NW + 1
    tile_range = jnp.arange(tile_count, dtype=jnp.int32)
    row_range = jnp.arange(TROWS, dtype=jnp.int32)

    strip_range = jnp.arange(tile_count * TROWS, dtype=jnp.int32)
    target = block_tile * TROWS + block_row
    counts_out = jnp.sum((target[None, :] == strip_range[:, None]).astype(jnp.int32), axis=1)
    place = gal_tile * depth + rank_before(gal_tile)
    word = (gal_row * columns + gal_col) * span + gal_shift
    slot_range = jnp.arange(tile_count * depth, dtype=jnp.int32)
    words_out = jnp.sum(
        jnp.where(place[None, :] == slot_range[:, None], word[None, :], 0), axis=1
    )
    sent = jnp.concatenate(
        [counts_out.reshape(tile_count, TROWS), words_out.reshape(tile_count, depth)], axis=1
    )
    got = lax.all_to_all(sent, "tile", split_axis=0, concat_axis=0, tiled=True)
    counts = jnp.sum(got[:, :TROWS], axis=0).astype(F32)
    words = got[:, TROWS:].reshape(-1)
    slot_shift = words % span
    slot_col = (words // span) % columns
    slot_row = words // (span * columns)

    reduce_rows = tile_row_sums if tile_count == 16 else tile_row_sums_any
    row_sums = reduce_rows(exposure_pixels, block_band, block_tile, block_row, band_weights)
    coadded = (row_sums / jnp.maximum(counts, 1.0)[:, None, None]).astype(BF16)
    matched_cube = psf_match(coadded, psf_kernel)

    column_range = jnp.arange(columns, dtype=jnp.int32)
    chosen = (
        (slot_row[None, None, :] == row_range[:, None, None])
        & (slot_col[None, None, :] == column_range[None, :, None])
    ).astype(BF16)
    spectra = lax.dot_general(
        matched_cube, chosen, (((0, 2), (0, 1)), ((), ())), preferred_element_type=F32
    )
    window = jnp.arange(NW, dtype=jnp.int32)
    channel_range = jnp.arange(channels, dtype=jnp.int32)
    inside = channel_range[None, :, None] == (slot_shift[None, :] + window[:, None])[:, None, :]
    values = jnp.sum(jnp.where(inside, spectra[None], 0.0), axis=1).T.astype(BF16)
    returned = lax.all_to_all(values, "tile", split_axis=0, concat_axis=0, tiled=True)
    mine = (place[:, None] == slot_range[None, :]).astype(BF16)
    rest_spectra = jnp.dot(mine, returned, preferred_element_type=F32).astype(BF16)
    return matched_cube, rest_spectra


def solution(mesh):
    one = P(("groups", "tile"))
    cube = P(("groups", "tile"), None, None)
    return jax.shard_map(
        body,
        mesh=mesh,
        in_specs=(cube, one, one, one, P(), P(), one, one, one, one),
        out_specs=(cube, P(("groups", "tile"), None)),
        check_vma=False,
    )
```

time: 392 us -> 141 us (0.36)
  blocking collectives: 149 us -> 13.9 us
  local copies, waits for them, and re-layouts: 121 us -> 9.22 us
  starting transfers between devices: 16.3 us -> 39.4 us
  matrix products: 19.5 us -> 1.14 us
  between operations: 15 us -> 1.24 us
  waiting for transfers between devices: 59.9 us -> 50.8 us
  Pallas kernels: 0 us -> 8.65 us
  other arithmetic: 9.58 us -> 16.1 us
    unnamed x1 -> x0, blocking collectives: 149 us -> none
    reduce_scatter x1 -> x0, waiting for transfers between devices: 56.6 us -> none  [body(): lax.psum_scatter(partial_value, 'tile', scatter_dimension=0, tiled=True)]
    gather x4 -> x0, local copies, waits for them, and re-layouts: 53.5 us -> none  [the longest x3 50.3 us: body(): jnp.take_along_axis(spectra_at, channel_window, axis=1).astype(jnp.bfloat16)]
    ppermute x2 -> x20, waiting for transfers between devices: 3.27 us -> 44.5 us  [the longest x2 32.6 us: tile_row_sums(): crossed.append(lax.ppermute(chip, 'tile', other_x))]
    scatter x6 -> x0, local copies, waits for them, and re-layouts: 34.1 us -> none  [the longest x1 19 us: body(): jnp.zeros((slot_count, channels, columns), jnp.bfloat16).at[slot_index]]
    ppermute x2 -> x20, starting transfers between devices: 2.76 us -> 32 us  [the longest x6 20.9 us: tile_row_sums(): up = lax.ppermute(up_term.astype(BF16), 'tile', forward)]
    dot_general x5 -> x2, matrix products: 19.5 us -> 1.14 us  [the longest x1 0.8 us: body(): jnp.dot(mine, returned, preferred_element_type=F32).astype(BF16)]
    all_to_all x0 -> x1, blocking collectives: none -> 13.9 us  [body(): lax.all_to_all(values, 'tile', split_axis=0, concat_axis=0, tiled=True)]
  transfers between devices with their start and end apart: 5 -> 21, of which waited for: 2 -> 8; matrix products, arithmetic and copies ran while one was open for 13% -> 8% of each run, Pallas kernels for 0% -> 0%
where the time goes in v1:
time: 141 us; the launch traced here: 140 us
  waiting for transfers between devices  50.8 us (36%)
  starting transfers between devices  39.4 us (28%)
  other arithmetic  16.1 us (11%)
  blocking collectives  13.9 us (10%)
  local copies, waits for them, and re-layouts  9.22 us (7%)
  Pallas kernels  8.65 us (6%)
    ppermute x2, waiting for transfers between devices, tile_row_sums(): crossed.append(lax.ppermute(chip, 'tile', other_x))  32.6 us
    ppermute x6, starting transfers between devices, tile_row_sums(): up = lax.ppermute(up_term.astype(BF16), 'tile', forward)  20.9 us
    all_to_all x1, blocking collectives, body(): lax.all_to_all(values, 'tile', split_axis=0, concat_axis=0, tiled=True)  13.9 us
    pallas_call x1, Pallas kernels, partial_sums(): pl.pallas_call(partial_sums_kernel, out_shape=[jax.ShapeDtypeStruct((rows...  8.65 us
    all_to_all x1, starting transfers between devices, body(): got = lax.all_to_all(sent, 'tile', split_axis=0, concat_axis=0, tiled=True)  7.35 us
    ppermute x6, waiting for transfers between devices, tile_row_sums(): down = lax.ppermute(down_term.astype(BF16), 'tile', backward)  6.32 us
    all_to_all x1, waiting for transfers between devices, body(): got = lax.all_to_all(sent, 'tile', split_axis=0, concat_axis=0, tiled=True)  6.24 us
    convert_element_type x1, other arithmetic, psf_match(): return total.astype(BF16)  5.55 us
  transfers between devices with their start and end apart: 21, of which 8 were waited for; matrix products, arithmetic and copies ran while one was open for 8% of the time, Pallas kernels for 0%

profile of v1, /device:TPU:0, one launch (start us, length us, event | category | flops | bytes accessed | tf_op | source)
XLA Modules:
  0.0 140.5 jit_solution(9441676512971765705)
XLA Ops:
  0.7 1.7 %copy.72.weights_ref = bf16[6,102,64]{2,1,0:T(8,128)(2,1)} copy(bf16[6,102,64]{1,2,0:T(8,128)(2,1)} %param.14) | data formatting | bytes 156672 | tf_op args[4]
  4.6 8.7 %partial_sums.1 = (bf16[32,102,128]{2,1,0:T(8,128)(2,1)S(1)}, bf16[32,102,128]{2,1,0:T(8,128)(2,1)S(1)}, bf16[32,102,128]{2,1,0:T(8,128)(2,1)S(1)}, bf16[32,102,...) custom-call(s32[128]{0:T(128)S(1)} %get-tuple-element.65.place_ref, ...), custom_call_target="tpu_custom_call" | custom-call | tf_op jit(solution)/shard_map/partial_sums/pallas_call | solution.py:57
  13.3 1.1 copy.75
  14.8 1.0 copy.73
  16.0 1.1 copy.88
  17.5 1.0 copy.86
  19.9 7.4 %all-to-all-start = ((s32[16,1,24]{2,1,0:T(1,128)}), s32[16,1,24]{2,1,0:T(1,128)S(1)}, u32[]{:S(2)}, u32[]{:S(2)}) async-start(s32[16,1,24]{2,1,0:T(1,128)} %bitcast.17), calls=%async_computation | async-start | bytes 16384 | tf_op jit(solution)/shard_map/all_to_all | solution.py:185
  27.4 6.2 %all-to-all-done = s32[16,1,24]{2,1,0:T(1,128)S(1)} async-done(((s32[16,1,24]{2,1,0:T(1,128)}), s32[16,1,24]{2,1,0:T(1,128)S(1)}, u32[]{:S(2)}, u32[]{:S(2)}) %all-to-all-start) | async-done | bytes 1568 | tf_op jit(solution)/shard_map/all_to_all | solution.py:185
  34.3 1.5 %add_convert_fusion.3 = bf16[32,102,128]{2,1,0:T(8,128)(2,1)S(1)} fusion(bf16[32,102,128]{2,1,0:T(8,128)(2,1)S(1)} %get-tuple-element.12, bf16[32,102,128]{2,0,1:T(8,128)(2,1)} %collective-permute-done.1), kind=kLoop, calls=%fused_computation.8 | loop fusion | flops 1671168 | bytes 2506752 | tf_op jit(solution)/shard_map/convert_element_type | solution.py:87
  36.5 1.5 %add_convert_fusion.1 = bf16[32,102,128]{2,1,0:T(8,128)(2,1)S(1)} fusion(bf16[32,102,128]{2,1,0:T(8,128)(2,1)S(1)} %get-tuple-element.16, bf16[32,102,128]{2,0,1:T(8,128)(2,1)} %collective-permute-done.10), kind=kLoop, calls=%fused_computation.6 | loop fusion | flops 1671168 | bytes 2506752 | tf_op jit(solution)/shard_map/convert_element_type | solution.py:87
  38.2 1.6 %collective-permute-start.11 = (bf16[32,102,128]{2,0,1:T(8,128)(2,1)S(1)}, bf16[32,102,128]{2,0,1:T(8,128)(2,1)S(1)}, u32[]{:S(2)}, u32[]{:S(2)}) collective-permute-start(bf16[32,102,128]{2,0,1:T(8,128)(2,1)S(1)} %copy.90), channel_id=1, source_target_pairs={{0,2},{1,3},{2,0},{3,1},{4,6},{5,7},{6,4},{7,5},{8,10},{9,11},{10,... | collective-permute-start | bytes 2506760 | tf_op jit(solution)/shard_map/ppermute | solution.py:88
  39.8 17.7 %collective-permute-done.2 = bf16[32,102,128]{2,0,1:T(8,128)(2,1)S(1)} collective-permute-done((bf16[32,102,128]{2,0,1:T(8,128)(2,1)S(1)}, bf16[32,102,128]{2,0,1:T(8,128)(2,1)S(1)}, u32[]{:S(2)}, u32[]{:S(2)}) %collective-permute-start.2) | collective-permute-done | bytes 835616 | tf_op jit(solution)/shard_map/ppermute | solution.py:88
  57.5 1.7 %add_convert_fusion.2 = bf16[32,102,128]{2,1,0:T(8,128)(2,1)S(1)} fusion(bf16[32,102,128]{2,1,0:T(8,128)(2,1)S(1)} %get-tuple-element.10, bf16[32,102,128]{2,0,1:T(8,128)(2,1)S(1)} %collective-permute-done.2, bf16[32,102,128]{2,0,1:T(8,128)(2,1)} %collective-permute-done), kind=kLoop, calls=%fused_computation.7 | loop fusion | flops 2506752 | bytes 3342336 | tf_op jit(solution)/shard_map/convert_element_type | solution.py:91
  59.2 15.0 %collective-permute-done.11 = bf16[32,102,128]{2,0,1:T(8,128)(2,1)S(1)} collective-permute-done((bf16[32,102,128]{2,0,1:T(8,128)(2,1)S(1)}, bf16[32,102,128]{2,0,1:T(8,128)(2,1)S(1)}, u32[]{:S(2)}, u32[]{:S(2)}) %collective-permute-start.11) | collective-permute-done | bytes 835616 | tf_op jit(solution)/shard_map/ppermute | solution.py:88
  74.2 1.7 %add_convert_fusion = bf16[32,102,128]{2,1,0:T(8,128)(2,1)S(1)} fusion(bf16[32,102,128]{2,1,0:T(8,128)(2,1)S(1)} %get-tuple-element.14, bf16[32,102,128]{2,0,1:T(8,128)(2,1)S(1)} %collective-permute-done.11, bf16[32,102,128]{2,0,1:T(8,128)(2,1)} %collective-permute-done.9), kind=kLoop, calls=%fused_computation.5 | loop fusion | flops 2506752 | bytes 3342336 | tf_op jit(solution)/shard_map/convert_element_type | solution.py:91
  76.3 2.5 %collective-permute-start.3 = (bf16[8,102,128]{2,0,1:T(8,128)(2,1)S(1)}, bf16[8,102,128]{2,0,1:T(8,128)(2,1)S(1)}, u32[]{:S(2)}, u32[]{:S(2)}) collective-permute-start(bf16[8,102,128]{2,0,1:T(8,128)(2,1)S(1)} %bitcast.130), channel_id=1, source_target_pairs={{0,4},{1,5},{2,6},{3,7},{16,20},{17,21},{18,22},{19,23}} | collective-permute-start | bytes 626696 | tf_op jit(solution)/shard_map/ppermute | solution.py:101
  79.5 1.3 collective-permute-start.12
  81.6 2.8 %collective-permute-done.3 = bf16[8,102,128]{2,0,1:T(8,128)(2,1)S(1)} collective-permute-done((bf16[8,102,128]{2,0,1:T(8,128)(2,1)S(1)}, bf16[8,102,128]{2,0,1:T(8,128)(2,1)S(1)}, u32[]{:S(2)}, u32[]{:S(2)}) %collective-permute-start.3) | collective-permute-done | bytes 208928 | tf_op jit(solution)/shard_map/ppermute | solution.py:101
  84.4 4.4 %collective-permute-start.4 = (bf16[8,102,128]{2,0,1:T(8,128)(2,1)S(1)}, bf16[8,102,128]{2,0,1:T(8,128)(2,1)S(1)}, u32[]{:S(2)}, u32[]{:S(2)}) collective-permute-start(bf16[8,102,128]{2,0,1:T(8,128)(2,1)S(1)} %fusion.20), channel_id=1, source_target_pairs={{0,4},{1,5},{2,6},{3,7},{4,8},{5,9},{6,10},{7,11},{16,20},{17,21},... | collective-permute-start | bytes 626696 | tf_op jit(solution)/shard_map/ppermute | solution.py:101
  89.6 3.4 %collective-permute-start.13 = (bf16[8,102,128]{2,0,1:T(8,128)(2,1)S(1)}, bf16[8,102,128]{2,0,1:T(8,128)(2,1)S(1)}, u32[]{:S(2)}, u32[]{:S(2)}) collective-permute-start(bf16[8,102,128]{2,0,1:T(8,128)(2,1)S(1)} %fusion.15), channel_id=1, source_target_pairs={{0,4},{1,5},{2,6},{3,7},{4,8},{5,9},{6,10},{7,11},{16,20},{17,21},... | collective-permute-start | bytes 626696 | tf_op jit(solution)/shard_map/ppermute | solution.py:101
  94.0 4.4 %collective-permute-start.5 = (bf16[8,102,128]{2,0,1:T(8,128)(2,1)S(1)}, bf16[8,102,128]{2,0,1:T(8,128)(2,1)S(1)}, u32[]{:S(2)}, u32[]{:S(2)}) collective-permute-start(bf16[8,102,128]{2,0,1:T(8,128)(2,1)S(1)} %fusion.21), channel_id=1, source_target_pairs={{0,4},{1,5},{2,6},{3,7},{4,8},{5,9},{6,10},{7,11},{8,12},{9,13},{1... | collective-permute-start | bytes 626696 | tf_op jit(solution)/shard_map/ppermute | solution.py:101
  98.5 1.3 collective-permute-start.8
  99.8 4.9 %collective-permute-start.14 = (bf16[8,102,128]{2,0,1:T(8,128)(2,1)S(1)}, bf16[8,102,128]{2,0,1:T(8,128)(2,1)S(1)}, u32[]{:S(2)}, u32[]{:S(2)}) collective-permute-start(bf16[8,102,128]{2,0,1:T(8,128)(2,1)S(1)} %fusion.16), channel_id=1, source_target_pairs={{0,4},{1,5},{2,6},{3,7},{4,8},{5,9},{6,10},{7,11},{8,12},{9,13},{1... | collective-permute-start | bytes 626696 | tf_op jit(solution)/shard_map/ppermute | solution.py:101
  104.8 1.3 collective-permute-start.17
  106.2 2.3 %collective-permute-done.8 = bf16[8,102,128]{2,0,1:T(8,128)(2,1)S(1)} collective-permute-done((bf16[8,102,128]{2,0,1:T(8,128)(2,1)S(1)}, bf16[8,102,128]{2,0,1:T(8,128)(2,1)S(1)}, u32[]{:S(2)}, u32[]{:S(2)}) %collective-permute-start.8) | collective-permute-done | bytes 208928 | tf_op jit(solution)/shard_map/ppermute | solution.py:102
  108.5 4.1 %collective-permute-done.17 = bf16[8,102,128]{2,0,1:T(8,128)(2,1)S(1)} collective-permute-done((bf16[8,102,128]{2,0,1:T(8,128)(2,1)S(1)}, bf16[8,102,128]{2,0,1:T(8,128)(2,1)S(1)}, u32[]{:S(2)}, u32[]{:S(2)}) %collective-permute-start.17) | collective-permute-done | bytes 208928 | tf_op jit(solution)/shard_map/ppermute | solution.py:102
  112.8 1.3 collective-permute-start.18
  114.1 1.3 collective-permute-start.19
  115.5 2.6 %collective-permute-done.19 = bf16[2,102,128]{2,0,1:T(2,128)(2,1)S(1)} collective-permute-done((bf16[2,102,128]{2,0,1:T(2,128)(2,1)S(1)}, bf16[2,102,128]{2,0,1:T(2,128)(2,1)S(1)}, u32[]{:S(2)}, u32[]{:S(2)}) %collective-permute-start.19) | collective-permute-done | bytes 52256 | tf_op jit(solution)/shard_map/ppermute | solution.py:136
  118.1 1.1 fusion.5
  119.1 5.5 %add_convert_fusion.4 = bf16[16,102,128]{2,0,1:T(8,128)(2,1)S(1)} fusion(bf16[16,102,128]{2,0,1:T(8,128)(2,1)S(1)} %fusion.7, bf16[2,102,128]{2,0,1:T(2,128)(2,1)S(1)} %collective-permute-done.19, bf16[2,102,128]{2,0,1:T(2,128)(2,1)S(1)} %collective-permute-done.18, bf16[20,102,132]{2,0,1:T(8,128)(2,1)S(1)} %fusion.5, f32[102]{0:T(128)S(1)} %get-tuple-element.57, ...), kind=kLoop, calls=%fused_computation.19 | loop fusion | flops 18173952 | bytes 9306072 | tf_op jit(solution)/shard_map/convert_element_type | solution.py:150
  125.7 13.9 %all_to_all.24 = bf16[16,2,256]{2,1,0:T(2,128)(2,1)S(1)} all-to-all(bf16[16,2,256]{2,1,0:T(2,128)(2,1)S(1)} %reshape.222), channel_id=1, replica_groups=mesh['groups'=2,'tile'=16] {'tile'}, dimensions={0} | all-to-all | bytes 32768 | tf_op jit(solution)/shard_map/all_to_all | solution.py:209
  (90 shorter events, 12.0 us)
Async XLA Ops:
  3.1 0.9 copy-start
  4.0 0.7 copy-start.1
  13.3 2.7 %copy-start.2 = (bf16[32,102,128]{2,1,0:T(8,128)(2,1)S(1)}, bf16[32,102,128]{2,1,0:T(8,128)(2,1)}, u32[]{:S(2)}) copy-start(bf16[32,102,128]{2,1,0:T(8,128)(2,1)} %get-tuple-element.17) | copy-start | bytes 2506756
  14.4 19.9 %collective-permute-start.1 = (bf16[32,102,128]{2,0,1:T(8,128)(2,1)}, bf16[32,102,128]{2,0,1:T(8,128)(2,1)}, u32[]{:S(2)}, u32[]{:S(2)}) collective-permute-start(bf16[32,102,128]{2,0,1:T(8,128)(2,1)} %copy.75), channel_id=1, source_target_pairs={{0,1},{1,0},{2,3},{3,2},{4,5},{5,4},{6,7},{7,6},{8,9},{9,8},{10,11... | collective-permute-start | bytes 2506760 | tf_op jit(solution)/shard_map/ppermute | solution.py:83
  15.9 2.9 %copy-start.8 = (s32[64]{0:T(128)S(1)}, s32[64]{0:T(128)}, u32[]{:S(2)}) copy-start(s32[64]{0:T(128)} %param.16) | copy-start | bytes 772
  15.9 3.1 %copy-start.5 = (s32[64]{0:T(128)S(1)}, s32[64]{0:T(128)}, u32[]{:S(2)}) copy-start(s32[64]{0:T(128)} %param.19) | copy-start | bytes 772
  15.9 3.1 %copy-start.6 = (s32[64]{0:T(128)S(1)}, s32[64]{0:T(128)}, u32[]{:S(2)}) copy-start(s32[64]{0:T(128)} %param.18) | copy-start | bytes 772
  15.9 3.2 %copy-start.7 = (s32[64]{0:T(128)S(1)}, s32[64]{0:T(128)}, u32[]{:S(2)}) copy-start(s32[64]{0:T(128)} %param.17) | copy-start | bytes 772
  15.9 23.9 %collective-permute-start = (bf16[32,102,128]{2,0,1:T(8,128)(2,1)}, bf16[32,102,128]{2,0,1:T(8,128)(2,1)}, u32[]{:S(2)}, u32[]{:S(2)}) collective-permute-start(bf16[32,102,128]{2,0,1:T(8,128)(2,1)} %copy.73), channel_id=1, source_target_pairs={{0,1},{1,0},{2,3},{3,2},{4,5},{5,4},{6,7},{7,6},{8,9},{9,8},{10,11... | collective-permute-start | bytes 2506760 | tf_op jit(solution)/shard_map/ppermute | solution.py:83
  16.0 11.3 %copy-start.4 = (f32[102,25]{0,1:T(8,128)S(1)}, f32[102,25]{0,1:T(8,128)}, u32[]{:S(2)}) copy-start(f32[102,25]{0,1:T(8,128)} %param.15) | copy-start | bytes 30604
  17.1 19.4 %collective-permute-start.10 = (bf16[32,102,128]{2,0,1:T(8,128)(2,1)}, bf16[32,102,128]{2,0,1:T(8,128)(2,1)}, u32[]{:S(2)}, u32[]{:S(2)}) collective-permute-start(bf16[32,102,128]{2,0,1:T(8,128)(2,1)} %copy.88), channel_id=1, source_target_pairs={{0,1},{1,0},{2,3},{3,2},{4,5},{5,4},{6,7},{7,6},{8,9},{9,8},{10,11... | collective-permute-start | bytes 2506760 | tf_op jit(solution)/shard_map/ppermute | solution.py:83
  18.6 40.7 %collective-permute-start.9 = (bf16[32,102,128]{2,0,1:T(8,128)(2,1)}, bf16[32,102,128]{2,0,1:T(8,128)(2,1)}, u32[]{:S(2)}, u32[]{:S(2)}) collective-permute-start(bf16[32,102,128]{2,0,1:T(8,128)(2,1)} %copy.86), channel_id=1, source_target_pairs={{0,1},{1,0},{2,3},{3,2},{4,5},{5,4},{6,7},{7,6},{8,9},{9,8},{10,11... | collective-permute-start | bytes 2506760 | tf_op jit(solution)/shard_map/ppermute | solution.py:83
  19.9 13.7 %all-to-all-start = ((s32[16,1,24]{2,1,0:T(1,128)}), s32[16,1,24]{2,1,0:T(1,128)S(1)}, u32[]{:S(2)}, u32[]{:S(2)}) async-start(s32[16,1,24]{2,1,0:T(1,128)} %bitcast.17), calls=%async_computation | async-start | bytes 16384 | tf_op jit(solution)/shard_map/all_to_all | solution.py:185
  35.9 21.6 %collective-permute-start.2 = (bf16[32,102,128]{2,0,1:T(8,128)(2,1)S(1)}, bf16[32,102,128]{2,0,1:T(8,128)(2,1)S(1)}, u32[]{:S(2)}, u32[]{:S(2)}) collective-permute-start(bf16[32,102,128]{2,0,1:T(8,128)(2,1)S(1)} %copy.77), channel_id=1, source_target_pairs={{0,2},{1,3},{2,0},{3,1},{4,6},{5,7},{6,4},{7,5},{8,10},{9,11},{10,... | collective-permute-start | bytes 2506760 | tf_op jit(solution)/shard_map/ppermute | solution.py:88
  38.2 36.0 %collective-permute-start.11 = (bf16[32,102,128]{2,0,1:T(8,128)(2,1)S(1)}, bf16[32,102,128]{2,0,1:T(8,128)(2,1)S(1)}, u32[]{:S(2)}, u32[]{:S(2)}) collective-permute-start(bf16[32,102,128]{2,0,1:T(8,128)(2,1)S(1)} %copy.90), channel_id=1, source_target_pairs={{0,2},{1,3},{2,0},{3,1},{4,6},{5,7},{6,4},{7,5},{8,10},{9,11},{10,... | collective-permute-start | bytes 2506760 | tf_op jit(solution)/shard_map/ppermute | solution.py:88
  76.3 8.1 %collective-permute-start.3 = (bf16[8,102,128]{2,0,1:T(8,128)(2,1)S(1)}, bf16[8,102,128]{2,0,1:T(8,128)(2,1)S(1)}, u32[]{:S(2)}, u32[]{:S(2)}) collective-permute-start(bf16[8,102,128]{2,0,1:T(8,128)(2,1)S(1)} %bitcast.130), channel_id=1, source_target_pairs={{0,4},{1,5},{2,6},{3,7},{16,20},{17,21},{18,22},{19,23}} | collective-permute-start | bytes 626696 | tf_op jit(solution)/shard_map/ppermute | solution.py:101
  78.8 10.0 %collective-permute-start.6 = (bf16[8,102,128]{2,0,1:T(8,128)(2,1)S(1)}, bf16[8,102,128]{2,0,1:T(8,128)(2,1)S(1)}, u32[]{:S(2)}, u32[]{:S(2)}) collective-permute-start(bf16[8,102,128]{2,0,1:T(8,128)(2,1)S(1)} %bitcast.129), channel_id=1, source_target_pairs={{15,11},{14,10},{13,9},{12,8},{31,27},{30,26},{29,25},{28,24}} | collective-permute-start | bytes 626696 | tf_op jit(solution)/shard_map/ppermute | solution.py:102
  79.5 10.0 %collective-permute-start.12 = (bf16[8,102,128]{2,0,1:T(8,128)(2,1)S(1)}, bf16[8,102,128]{2,0,1:T(8,128)(2,1)S(1)}, u32[]{:S(2)}, u32[]{:S(2)}) collective-permute-start(bf16[8,102,128]{2,0,1:T(8,128)(2,1)S(1)} %bitcast.128), channel_id=1, source_target_pairs={{0,4},{1,5},{2,6},{3,7},{16,20},{17,21},{18,22},{19,23}} | collective-permute-start | bytes 626696 | tf_op jit(solution)/shard_map/ppermute | solution.py:101
  80.9 12.2 %collective-permute-start.15 = (bf16[8,102,128]{2,0,1:T(8,128)(2,1)S(1)}, bf16[8,102,128]{2,0,1:T(8,128)(2,1)S(1)}, u32[]{:S(2)}, u32[]{:S(2)}) collective-permute-start(bf16[8,102,128]{2,0,1:T(8,128)(2,1)S(1)} %bitcast.127), channel_id=1, source_target_pairs={{15,11},{14,10},{13,9},{12,8},{31,27},{30,26},{29,25},{28,24}} | collective-permute-start | bytes 626696 | tf_op jit(solution)/shard_map/ppermute | solution.py:102
  84.4 9.5 %collective-permute-start.4 = (bf16[8,102,128]{2,0,1:T(8,128)(2,1)S(1)}, bf16[8,102,128]{2,0,1:T(8,128)(2,1)S(1)}, u32[]{:S(2)}, u32[]{:S(2)}) collective-permute-start(bf16[8,102,128]{2,0,1:T(8,128)(2,1)S(1)} %fusion.20), channel_id=1, source_target_pairs={{0,4},{1,5},{2,6},{3,7},{4,8},{5,9},{6,10},{7,11},{16,20},{17,21},... | collective-permute-start | bytes 626696 | tf_op jit(solution)/shard_map/ppermute | solution.py:101
  88.9 9.5 %collective-permute-start.7 = (bf16[8,102,128]{2,0,1:T(8,128)(2,1)S(1)}, bf16[8,102,128]{2,0,1:T(8,128)(2,1)S(1)}, u32[]{:S(2)}, u32[]{:S(2)}) collective-permute-start(bf16[8,102,128]{2,0,1:T(8,128)(2,1)S(1)} %fusion.18), channel_id=1, source_target_pairs={{15,11},{14,10},{13,9},{12,8},{11,7},{10,6},{9,5},{8,4},{31,27},{3... | collective-permute-start | bytes 626696 | tf_op jit(solution)/shard_map/ppermute | solution.py:102
  89.6 10.2 %collective-permute-start.13 = (bf16[8,102,128]{2,0,1:T(8,128)(2,1)S(1)}, bf16[8,102,128]{2,0,1:T(8,128)(2,1)S(1)}, u32[]{:S(2)}, u32[]{:S(2)}) collective-permute-start(bf16[8,102,128]{2,0,1:T(8,128)(2,1)S(1)} %fusion.15), channel_id=1, source_target_pairs={{0,4},{1,5},{2,6},{3,7},{4,8},{5,9},{6,10},{7,11},{16,20},{17,21},... | collective-permute-start | bytes 626696 | tf_op jit(solution)/shard_map/ppermute | solution.py:101
  93.1 11.7 %collective-permute-start.16 = (bf16[8,102,128]{2,0,1:T(8,128)(2,1)S(1)}, bf16[8,102,128]{2,0,1:T(8,128)(2,1)S(1)}, u32[]{:S(2)}, u32[]{:S(2)}) collective-permute-start(bf16[8,102,128]{2,0,1:T(8,128)(2,1)S(1)} %fusion.13), channel_id=1, source_target_pairs={{15,11},{14,10},{13,9},{12,8},{11,7},{10,6},{9,5},{8,4},{31,27},{3... | collective-permute-start | bytes 626696 | tf_op jit(solution)/shard_map/ppermute | solution.py:102
  94.0 12.1 %collective-permute-start.5 = (bf16[8,102,128]{2,0,1:T(8,128)(2,1)S(1)}, bf16[8,102,128]{2,0,1:T(8,128)(2,1)S(1)}, u32[]{:S(2)}, u32[]{:S(2)}) collective-permute-start(bf16[8,102,128]{2,0,1:T(8,128)(2,1)S(1)} %fusion.21), channel_id=1, source_target_pairs={{0,4},{1,5},{2,6},{3,7},{4,8},{5,9},{6,10},{7,11},{8,12},{9,13},{1... | collective-permute-start | bytes 626696 | tf_op jit(solution)/shard_map/ppermute | solution.py:101
  98.5 9.9 %collective-permute-start.8 = (bf16[8,102,128]{2,0,1:T(8,128)(2,1)S(1)}, bf16[8,102,128]{2,0,1:T(8,128)(2,1)S(1)}, u32[]{:S(2)}, u32[]{:S(2)}) collective-permute-start(bf16[8,102,128]{2,0,1:T(8,128)(2,1)S(1)} %fusion.19), channel_id=1, source_target_pairs={{15,11},{14,10},{13,9},{12,8},{11,7},{10,6},{9,5},{8,4},{7,3},{6,2... | collective-permute-start | bytes 626696 | tf_op jit(solution)/shard_map/ppermute | solution.py:102
  99.8 8.6 %collective-permute-start.14 = (bf16[8,102,128]{2,0,1:T(8,128)(2,1)S(1)}, bf16[8,102,128]{2,0,1:T(8,128)(2,1)S(1)}, u32[]{:S(2)}, u32[]{:S(2)}) collective-permute-start(bf16[8,102,128]{2,0,1:T(8,128)(2,1)S(1)} %fusion.16), channel_id=1, source_target_pairs={{0,4},{1,5},{2,6},{3,7},{4,8},{5,9},{6,10},{7,11},{8,12},{9,13},{1... | collective-permute-start | bytes 626696 | tf_op jit(solution)/shard_map/ppermute | solution.py:101
  104.8 7.7 %collective-permute-start.17 = (bf16[8,102,128]{2,0,1:T(8,128)(2,1)S(1)}, bf16[8,102,128]{2,0,1:T(8,128)(2,1)S(1)}, u32[]{:S(2)}, u32[]{:S(2)}) collective-permute-start(bf16[8,102,128]{2,0,1:T(8,128)(2,1)S(1)} %fusion.14), channel_id=1, source_target_pairs={{15,11},{14,10},{13,9},{12,8},{11,7},{10,6},{9,5},{8,4},{7,3},{6,2... | collective-permute-start | bytes 626696 | tf_op jit(solution)/shard_map/ppermute | solution.py:102
  112.8 2.6 %collective-permute-start.18 = (bf16[2,102,128]{2,0,1:T(2,128)(2,1)S(1)}, bf16[2,102,128]{2,0,1:T(2,128)(2,1)S(1)}, u32[]{:S(2)}, u32[]{:S(2)}) collective-permute-start(bf16[2,102,128]{2,0,1:T(2,128)(2,1)S(1)} %get-tuple-element.32), channel_id=1, source_target_pairs={{0,1},{1,2},{2,3},{3,4},{4,5},{5,6},{6,7},{7,8},{8,9},{9,10},{10,1... | collective-permute-start | bytes 156680 | tf_op jit(solution)/shard_map/ppermute | solution.py:135
  114.1 3.9 %collective-permute-start.19 = (bf16[2,102,128]{2,0,1:T(2,128)(2,1)S(1)}, bf16[2,102,128]{2,0,1:T(2,128)(2,1)S(1)}, u32[]{:S(2)}, u32[]{:S(2)}) collective-permute-start(bf16[2,102,128]{2,0,1:T(2,128)(2,1)S(1)} %get-tuple-element.33), channel_id=1, source_target_pairs={{1,0},{2,1},{3,2},{4,3},{5,4},{6,5},{7,6},{8,7},{9,8},{10,9},{11,1... | collective-permute-start | bytes 156680 | tf_op jit(solution)/shard_map/ppermute | solution.py:136
  124.7 15.8 %copy-start.3 = (bf16[16,102,128]{2,0,1:T(8,128)(2,1)}, bf16[16,102,128]{2,0,1:T(8,128)(2,1)S(1)}, u32[]{:S(2)}) copy-start(bf16[16,102,128]{2,0,1:T(8,128)(2,1)S(1)} %add_convert_fusion.4) | copy-start | bytes 1253380

commit v2 on v1

--- a/solution.py
+++ b/solution.py
@@ -1,5 +1,3 @@
-import functools
-
 import jax
 import jax.numpy as jnp
 from jax import lax
@@ -12,14 +10,14 @@
 TROWS = 16
 F32 = jnp.float32
 BF16 = jnp.bfloat16
-CHUNKS = 2
+CHUNKS = 4
+MESH = pl.DeviceIdType.MESH
 GROUP = 8
 
 
-def partial_sums_kernel(place_ref, band_ref, pixels_ref, weights_ref, *rest):
-    outs, total = rest[:-1], rest[-1]
+def partial_sums_kernel(place_ref, band_ref, pixels_ref, weights_ref, keep_ref, send_ref, total):
     blocks = pixels_ref.shape[0]
-    rows_out = outs[0].shape[0]
+    half = total.shape[0] // 2
 
     def clear(i, _):
         total[i] = jnp.zeros(total.shape[1:], F32)
@@ -41,67 +39,371 @@
 
     lax.fori_loop(0, blocks // GROUP, step, 0)
 
-    for n, out in enumerate(outs):
-
-        def emit(i, _, n=n, out=out):
-            out[i] = total[n * rows_out + i].astype(BF16)
-            return 0
-
-        lax.fori_loop(0, rows_out, emit, 0, unroll=4)
-
-
-def partial_sums(place, band, pixels, weights, rows, pieces):
+    def emit(i, _):
+        keep_ref[i] = total[i].astype(BF16)
+        send_ref[i] = total[half + i].astype(BF16)
+        return 0
+
+    lax.fori_loop(0, half, emit, 0, unroll=4)
+
+
+def partial_sums(place, band, pixels, weights, rows):
     channels, columns = weights.shape[1], pixels.shape[2]
     smem = pl.BlockSpec(memory_space=pltpu.SMEM)
     vmem = pl.BlockSpec(memory_space=pltpu.VMEM)
     return pl.pallas_call(
         partial_sums_kernel,
-        out_shape=[jax.ShapeDtypeStruct((rows // pieces, channels, columns), BF16)] * pieces,
+        out_shape=[jax.ShapeDtypeStruct((rows // 2, channels, columns), BF16)] * 2,
         in_specs=[smem, smem, vmem, vmem],
-        out_specs=[vmem] * pieces,
+        out_specs=[vmem] * 2,
         scratch_shapes=[pltpu.VMEM((rows, channels, columns), F32)],
-        compiler_params=pltpu.CompilerParams(vmem_limit_bytes=48 * 1024 * 1024),
+        compiler_params=pltpu.CompilerParams(vmem_limit_bytes=40 * 1024 * 1024),
         name="partial_sums",
     )(place, band, pixels, weights)
 
 
-def tile_row_sums(pixels, band, tile, row, weights):
+def greet_all(me, count):
+    barrier = pltpu.get_barrier_semaphore()
+
+    def hello(k, _):
+        pl.semaphore_signal(
+            barrier, inc=1, device_id={"tile": (me + k) % count}, device_id_type=MESH
+        )
+        return 0
+
+    lax.fori_loop(1, count, hello, 0)
+    pl.semaphore_wait(barrier, count - 1)
+
+
+def exchange_copy(k, me, count, out_ref, in_ref, send_sem, recv_sem):
+    there = (me + k) % count
+    return pltpu.make_async_remote_copy(
+        src_ref=out_ref.at[there],
+        dst_ref=in_ref.at[me],
+        send_sem=send_sem.at[k],
+        recv_sem=recv_sem.at[k],
+        device_id={"tile": there},
+        device_id_type=MESH,
+    )
+
+
+def reduce_kernel(
+    notes_ref, keep_ref, send_ref, rows_ref, notes_out_ref,
+    notes_in, from_core, to_x, from_x, plane, chain_out, chain_in, halo_in,
+    note_send, note_recv, core_send, core_recv, x_send, x_recv,
+    chain_send, chain_recv, halo_send, halo_recv,
+):
+    count = 16
     me = lax.axis_index("tile")
     z, x, c = me // 4, (me // 2) % 2, me % 2
+    other_core = me + 1 - 2 * c
+    other_x = me + 2 - 4 * x
+    part = TROWS // CHUNKS
+    size = 4 * part
+
+    def remote(src, dst, send_sem, recv_sem, there):
+        return pltpu.make_async_remote_copy(
+            src_ref=src, dst_ref=dst, send_sem=send_sem, recv_sem=recv_sem,
+            device_id={"tile": there}, device_id_type=MESH,
+        )
+
+    def core_copy(far, k):
+        at = far * CHUNKS + k
+        rows = pl.ds(at * size, size)
+        return remote(
+            send_ref.at[rows], from_core.at[rows], core_send.at[at], core_recv.at[at], other_core
+        )
+
+    def x_copy(k):
+        rows = pl.ds(k * size, size)
+        return remote(to_x.at[rows], from_x.at[rows], x_send.at[k], x_recv.at[k], other_x)
+
+    def chain_copy(way, k, dist):
+        at = (way * CHUNKS + k) * 3 + dist - 1
+        there = (me + 4) % count if way == 0 else (me + 12) % count
+        rows = pl.ds(at * part, part)
+        return remote(
+            chain_out.at[rows], chain_in.at[rows], chain_send.at[at], chain_recv.at[at], there
+        )
+
+    def note(k):
+        return exchange_copy(k, me, count, notes_ref, notes_in, note_send, note_recv)
+
+    greet_all(me, count)
+    for k in range(CHUNKS):
+        core_copy(1, k).start()
+
+    def send_note(k, _):
+        note(k).start()
+        return 0
+
+    lax.fori_loop(1, count, send_note, 0)
+
+    for k in range(CHUNKS):
+        core_copy(1, k).wait_recv()
+
+        def add_x(i, _, k=k):
+            at = (CHUNKS + k) * size + i
+            to_x[k * size + i] = (
+                keep_ref[at].astype(F32) + from_core[at].astype(F32)
+            ).astype(BF16)
+            return 0
+
+        lax.fori_loop(0, size, add_x, 0)
+        x_copy(k).start()
+    for k in range(CHUNKS):
+        core_copy(0, k).start()
+
+    def wait_note(k, total):
+        note(k).wait_recv()
+        return total
+
+    lax.fori_loop(1, count, wait_note, 0)
+    notes_in[me] = notes_ref[me]
+    notes_out_ref[...] = notes_in[:, TROWS:, :]
+    counts = jnp.maximum(jnp.sum(notes_in[:, :TROWS, :], axis=0).astype(F32), 1.0)
+
+    def sends(way, dist):
+        return z + dist <= 3 if way == 0 else z >= dist
+
+    def receives(way, dist):
+        if way == 0:
+            return jnp.logical_and(z >= 1, z + dist <= 4)
+        return jnp.logical_and(z <= 2, z >= dist - 1)
+
+    def hop(k, dist):
+        for way in range(2):
+
+            @pl.when(sends(way, dist))
+            def _(way=way):
+                to_z = z + dist if way == 0 else z - dist
+                at = ((way * CHUNKS + k) * 3 + dist - 1) * part
+                source = k * size + to_z * part
+                edge = z >= 1 if way == 0 else z <= 2
+                if dist == 3:
+                    def put(i, _):
+                        chain_out[at + i] = plane[source + i]
+                        return 0
+
+                    lax.fori_loop(0, part, put, 0)
+                else:
+                    @pl.when(edge)
+                    def _():
+                        chain_copy(way, k, dist + 1).wait_recv()
+
+                        def put(i, _):
+                            chain_out[at + i] = (
+                                plane[source + i].astype(F32)
+                                + chain_in[at + part + i].astype(F32)
+                            ).astype(BF16)
+                            return 0
+
+                        lax.fori_loop(0, part, put, 0)
+
+                    @pl.when(jnp.logical_not(edge))
+                    def _():
+                        def put(i, _):
+                            chain_out[at + i] = plane[source + i]
+                            return 0
+
+                        lax.fori_loop(0, part, put, 0)
+                chain_copy(way, k, dist).start()
+
+    def finish(k):
+        up_at, down_at = k * 3 * part, (CHUNKS + k) * 3 * part
+
+        @pl.when(receives(0, 1))
+        def _():
+            chain_copy(0, k, 1).wait_recv()
+
+        @pl.when(receives(1, 1))
+        def _():
+            chain_copy(1, k, 1).wait_recv()
+
+        up_on, down_on = z >= 1, z <= 2
+        for i in range(part):
+            value = plane[k * size + z * part + i].astype(F32)
+            value = value + jnp.where(up_on, chain_in[up_at + i].astype(F32), 0.0)
+            value = value + jnp.where(down_on, chain_in[down_at + i].astype(F32), 0.0)
+            row = k * part + i
+            rows_ref[2 + row] = (value / counts[row : row + 1, :]).astype(BF16)
+
+    def halo_copy(way):
+        rows = pl.ds(2, 2) if way == 0 else pl.ds(TROWS, 2)
+        there = (me + 15) % count if way == 0 else (me + 1) % count
+        return remote(
+            rows_ref.at[rows], halo_in.at[pl.ds(2 * way, 2)], halo_send.at[way],
+            halo_recv.at[way], there,
+        )
+
+    def done(k):
+        finish(k)
+        if k == 0:
+            @pl.when(me >= 1)
+            def _():
+                halo_copy(0).start()
+        if k == CHUNKS - 1:
+            @pl.when(me <= count - 2)
+            def _():
+                halo_copy(1).start()
+
+    for k in range(CHUNKS):
+        core_copy(0, k).wait_recv()
+        x_copy(k).wait_recv()
+
+        def add_plane(i, _, k=k):
+            at = k * size + i
+            plane[at] = (
+                keep_ref[at].astype(F32) + from_core[at].astype(F32) + from_x[at].astype(F32)
+            ).astype(BF16)
+            return 0
+
+        lax.fori_loop(0, size, add_plane, 0)
+        hop(k, 3)
+        if k > 0:
+            done(k - 1)
+        hop(k, 2)
+        hop(k, 1)
+    done(CHUNKS - 1)
+
+    for i in range(2):
+        rows_ref[i] = jnp.zeros(rows_ref.shape[1:], BF16)
+        rows_ref[TROWS + 2 + i] = jnp.zeros(rows_ref.shape[1:], BF16)
+
+    @pl.when(me <= count - 2)
+    def _():
+        halo_copy(0).wait_recv()
+        for i in range(2):
+            rows_ref[TROWS + 2 + i] = halo_in[i]
+
+    @pl.when(me >= 1)
+    def _():
+        halo_copy(1).wait_recv()
+        for i in range(2):
+            rows_ref[i] = halo_in[2 + i]
+
+    @pl.when(me >= 1)
+    def _():
+        halo_copy(0).wait_send()
+
+    @pl.when(me <= count - 2)
+    def _():
+        halo_copy(1).wait_send()
+
+    def wait_note_sent(k, _):
+        note(k).wait_send()
+        return 0
+
+    lax.fori_loop(1, count, wait_note_sent, 0)
+    for k in range(CHUNKS):
+        core_copy(1, k).wait_send()
+        core_copy(0, k).wait_send()
+        x_copy(k).wait_send()
+        for way in range(2):
+            for dist in (3, 2, 1):
+                @pl.when(sends(way, dist))
+                def _(way=way, k=k, dist=dist):
+                    chain_copy(way, k, dist).wait_send()
+
+
+def reduce_rows_and_notes(notes, keep, send):
+    tail = keep.shape[1:]
+    vmem = pl.BlockSpec(memory_space=pltpu.VMEM)
+    part = TROWS // CHUNKS
+    dma = pltpu.SemaphoreType.DMA
+    return pl.pallas_call(
+        reduce_kernel,
+        out_shape=[
+            jax.ShapeDtypeStruct((TROWS + 4,) + tail, BF16),
+            jax.ShapeDtypeStruct((16, notes.shape[1] - TROWS, 128), jnp.int32),
+        ],
+        in_specs=[vmem] * 3,
+        out_specs=[vmem] * 2,
+        scratch_shapes=[
+            pltpu.VMEM(notes.shape, jnp.int32),
+            pltpu.VMEM((8 * TROWS,) + tail, BF16),
+            pltpu.VMEM((4 * TROWS,) + tail, BF16),
+            pltpu.VMEM((4 * TROWS,) + tail, BF16),
+            pltpu.VMEM((4 * TROWS,) + tail, BF16),
+            pltpu.VMEM((6 * TROWS,) + tail, BF16),
+            pltpu.VMEM((6 * TROWS,) + tail, BF16),
+            pltpu.VMEM((4,) + tail, BF16),
+            dma((16,)), dma((16,)),
+            dma((2 * CHUNKS,)), dma((2 * CHUNKS,)),
+            dma((CHUNKS,)), dma((CHUNKS,)),
+            dma((6 * CHUNKS,)), dma((6 * CHUNKS,)),
+            dma((2,)), dma((2,)),
+        ],
+        compiler_params=pltpu.CompilerParams(
+            collective_id=0, has_side_effects=True, vmem_limit_bytes=40 * 1024 * 1024
+        ),
+        name="reduce_rows",
+    )(notes, keep, send)
+
+
+def exchange_kernel(out_ref, in_ref, landed, send_sem, recv_sem):
+    count = out_ref.shape[0]
+    me = lax.axis_index("tile")
+
+    def copy(k):
+        return exchange_copy(k, me, count, out_ref, landed, send_sem, recv_sem)
+
+    greet_all(me, count)
+
+    def start(k, _):
+        copy(k).start()
+        return 0
+
+    def wait(k, _):
+        copy(k).wait()
+        return 0
+
+    lax.fori_loop(1, count, start, 0)
+    landed[me] = out_ref[me]
+    lax.fori_loop(1, count, wait, 0)
+    in_ref[...] = landed[...]
+
+
+def exchange(values):
+    vmem = pl.BlockSpec(memory_space=pltpu.VMEM)
+    return pl.pallas_call(
+        exchange_kernel,
+        out_shape=jax.ShapeDtypeStruct(values.shape, values.dtype),
+        in_specs=[vmem],
+        out_specs=vmem,
+        scratch_shapes=[
+            pltpu.VMEM(values.shape, values.dtype),
+            pltpu.SemaphoreType.DMA((values.shape[0],)),
+            pltpu.SemaphoreType.DMA((values.shape[0],)),
+        ],
+        compiler_params=pltpu.CompilerParams(
+            collective_id=1, has_side_effects=True, vmem_limit_bytes=40 * 1024 * 1024
+        ),
+        name="exchange",
+    )(values)
+
+
+def averaged_rows(pixels, band, tile, row, weights, counts_out, words_out):
+    me = lax.axis_index("tile")
+    x, c = (me // 2) % 2, me % 2
     dest_z, dest_x, dest_c = tile // 4, (tile // 2) % 2, tile % 2
     far_x, far_c = (dest_x + x) % 2, (dest_c + c) % 2
     part = TROWS // CHUNKS
     place = (((far_c * 2 + far_x) * CHUNKS + row // part) * 4 + dest_z) * part + row % part
-    out = partial_sums(place, band, pixels, weights, 16 * TROWS, 4 * CHUNKS)
-    other_core = [(i, i ^ 1) for i in range(16)]
-    other_x = [(i, i ^ 2) for i in range(16)]
-    keep = lambda far, chunk: out[far * CHUNKS + chunk]
-    send = lambda far, chunk: out[(2 + far) * CHUNKS + chunk]
-    arrived = {}
-    for far in (1, 0):
-        for chunk in range(CHUNKS):
-            arrived[far, chunk] = lax.ppermute(send(far, chunk), "tile", other_core)
-    wide = lambda a: a.astype(F32)
-    crossed = []
-    for chunk in range(CHUNKS):
-        chip = (wide(keep(1, chunk)) + wide(arrived[1, chunk])).astype(BF16)
-        crossed.append(lax.ppermute(chip, "tile", other_x))
-    sums = []
-    for chunk in range(CHUNKS):
-        plane = (wide(keep(0, chunk)) + wide(arrived[0, chunk]) + wide(crossed[chunk])).astype(BF16)
-        plane = plane.reshape((4, part) + plane.shape[1:])
-        pick = lambda at: wide(lax.dynamic_index_in_dim(plane, jnp.clip(at, 0, 3), 0, keepdims=False))
-        up = down = None
-        for dist in (3, 2, 1):
-            up_term, down_term = pick(z + dist), pick(z - dist)
-            if up is not None:
-                up_term, down_term = up_term + wide(up), down_term + wide(down)
-            forward = [(i, i + 4) for i in range(4 * (4 - dist))]
-            backward = [(15 - i, 15 - j) for i, j in forward]
-            up = lax.ppermute(up_term.astype(BF16), "tile", forward)
-            down = lax.ppermute(down_term.astype(BF16), "tile", backward)
-        sums.append(pick(z) + wide(up) + wide(down))
-    return jnp.concatenate(sums, axis=0)
+    keep, send = partial_sums(place, band, pixels, weights, 16 * TROWS)
+    notes = jnp.concatenate([counts_out, words_out], axis=1)
+    notes = jnp.broadcast_to(notes[:, :, None], notes.shape + (128,))
+    rows, notes = reduce_rows_and_notes(notes, keep, send)
+    return rows, notes[:, :, 0].reshape(-1)
+
+
+def averaged_rows_any(pixels, band, tile, row, weights, counts_out, words_out):
+    sent = jnp.concatenate([counts_out, words_out], axis=1)
+    got = lax.all_to_all(sent, "tile", split_axis=0, concat_axis=0, tiled=True)
+    counts = jnp.sum(got[:, :TROWS], axis=0).astype(F32)
+    row_sums = tile_row_sums_any(pixels, band, tile, row, weights)
+    rows = (row_sums / jnp.maximum(counts, 1.0)[:, None, None]).astype(BF16)
+    return with_halo(rows, KW // 2), got[:, TROWS:].reshape(-1)
 
 
 def tile_row_sums_any(pixels, band, tile, row, weights):
@@ -140,7 +442,7 @@
 def psf_match(coadded, psf_kernel):
     radius = KW // 2
     columns = coadded.shape[2]
-    padded = jnp.pad(with_halo(coadded, radius), ((0, 0), (0, 0), (radius, radius)))
+    padded = jnp.pad(coadded, ((0, 0), (0, 0), (radius, radius)))
     total = None
     for dy in range(KW):
         for dx in range(KW):
@@ -179,19 +481,14 @@
     words_out = jnp.sum(
         jnp.where(place[None, :] == slot_range[:, None], word[None, :], 0), axis=1
     )
-    sent = jnp.concatenate(
-        [counts_out.reshape(tile_count, TROWS), words_out.reshape(tile_count, depth)], axis=1
+    small = tile_count == 16
+    coadded, words = (averaged_rows if small else averaged_rows_any)(
+        exposure_pixels, block_band, block_tile, block_row, band_weights,
+        counts_out.reshape(tile_count, TROWS), words_out.reshape(tile_count, depth),
     )
-    got = lax.all_to_all(sent, "tile", split_axis=0, concat_axis=0, tiled=True)
-    counts = jnp.sum(got[:, :TROWS], axis=0).astype(F32)
-    words = got[:, TROWS:].reshape(-1)
     slot_shift = words % span
     slot_col = (words // span) % columns
     slot_row = words // (span * columns)
-
-    reduce_rows = tile_row_sums if tile_count == 16 else tile_row_sums_any
-    row_sums = reduce_rows(exposure_pixels, block_band, block_tile, block_row, band_weights)
-    coadded = (row_sums / jnp.maximum(counts, 1.0)[:, None, None]).astype(BF16)
     matched_cube = psf_match(coadded, psf_kernel)
 
     column_range = jnp.arange(columns, dtype=jnp.int32)
@@ -206,7 +503,12 @@
     channel_range = jnp.arange(channels, dtype=jnp.int32)
     inside = channel_range[None, :, None] == (slot_shift[None, :] + window[:, None])[:, None, :]
     values = jnp.sum(jnp.where(inside, spectra[None], 0.0), axis=1).T.astype(BF16)
-    returned = lax.all_to_all(values, "tile", split_axis=0, concat_axis=0, tiled=True)
+    if small:
+        values = jnp.pad(values, ((0, 0), (0, 128 - NW))).astype(F32)
+        returned = exchange(values.reshape(tile_count, depth, 128))
+        returned = returned.reshape(-1, 128)[:, :NW].astype(BF16)
+    else:
+        returned = lax.all_to_all(values, "tile", split_axis=0, concat_axis=0, tiled=True)
     mine = (place[:, None] == slot_range[None, :]).astype(BF16)
     rest_spectra = jnp.dot(mine, returned, preferred_element_type=F32).astype(BF16)
     return matched_cube, rest_spectra

time: 141 us -> 99.5 us (0.71)
  Pallas kernels: 8.65 us -> 76.5 us
  waiting for transfers between devices: 50.8 us -> 0 us
  starting transfers between devices: 39.4 us -> 0 us
  blocking collectives: 13.9 us -> 0 us
  other arithmetic: 16.1 us -> 8.35 us
  local copies, waits for them, and re-layouts: 9.22 us -> 12.4 us
    pallas_call x0 -> x2, Pallas kernels: none -> 70 us  [the longest x1 60.1 us: reduce_rows_and_notes(): pl.pallas_call(reduce_kernel, out_shape=[jax.ShapeDtypeStruct((TROWS + 4,...]
    ppermute x20 -> x0, waiting for transfers between devices: 44.5 us -> none  [the longest x2 32.6 us: tile_row_sums(): crossed.append(lax.ppermute(chip, 'tile', other_x))]
    ppermute x20 -> x0, starting transfers between devices: 32 us -> none  [the longest x6 20.9 us: tile_row_sums(): up = lax.ppermute(up_term.astype(BF16), 'tile', forward)]
    all_to_all x1 -> x0, blocking collectives: 13.9 us -> none  [body(): lax.all_to_all(values, 'tile', split_axis=0, concat_axis=0, tiled=True)]
    unnamed x21 -> x16, local copies, waits for them, and re-layouts: 3.5 us -> 11.5 us
    all_to_all x1 -> x0, starting transfers between devices: 7.35 us -> none  [body(): got = lax.all_to_all(sent, 'tile', split_axis=0, concat_axis=0, tiled=True)]
    convert_element_type x13 -> x0, other arithmetic: 6.99 us -> none  [the longest x2 3.48 us: tile_row_sums(): (wide(keep(0, chunk)) + wide(arrived[0, chunk]) + wide(crossed[chunk])).a...]
    all_to_all x1 -> x0, waiting for transfers between devices: 6.24 us -> none  [body(): got = lax.all_to_all(sent, 'tile', split_axis=0, concat_axis=0, tiled=True)]
  transfers between devices with their start and end apart: 21 -> 0, of which waited for: 8 -> 0; matrix products, arithmetic and copies ran while one was open for 8% -> 0% of each run, Pallas kernels for 0% -> 0%
where the time goes in v2:
time: 99.5 us; the launch traced here: 99.2 us
  Pallas kernels  76.5 us (77%)
  local copies, waits for them, and re-layouts  12.4 us (12%)
  other arithmetic  8.35 us (8%)
  matrix products  1.09 us (1%)
    pallas_call x1, Pallas kernels, reduce_rows_and_notes(): pl.pallas_call(reduce_kernel, out_shape=[jax.ShapeDtypeStruct((TROWS + 4,...  60.1 us
    unnamed x16, local copies, waits for them, and re-layouts  11.5 us
    pallas_call x1, Pallas kernels, exchange(): pl.pallas_call(exchange_kernel, out_shape=jax.ShapeDtypeStruct(values.sha...  9.87 us
    pallas_call x1, Pallas kernels, partial_sums(): pl.pallas_call(partial_sums_kernel, out_shape=[jax.ShapeDtypeStruct((rows...  6.57 us
    convert_element_type x1, other arithmetic, psf_match(): return total.astype(BF16)  3.74 us

profile of v2, /device:TPU:0, one launch (start us, length us, event | category | flops | bytes accessed | tf_op | source)
XLA Modules:
  0.0 99.2 jit_solution(7167185357837617975)
XLA Ops:
  0.7 0.7 fusion.9
  1.4 1.1 %copy.16.weights_ref = bf16[6,102,64]{2,1,0:T(8,128)(2,1)S(1)} copy(bf16[6,102,64]{1,2,0:T(8,128)(2,1)} %param.14) | data formatting | bytes 156672 | tf_op args[4]
  2.4 1.6 %copy-done.4 = bf16[128,64,128]{2,1,0:T(8,128)(2,1)S(1)} copy-done((bf16[128,64,128]{2,1,0:T(8,128)(2,1)S(1)}, bf16[128,64,128]{2,1,0:T(8,128)(2,1)}, u32[]{:S(2)}) %copy-start.4) | copy-done | bytes 2097176
  4.0 0.7 copy-done.5
  4.7 6.6 %partial_sums.1 = (bf16[128,102,128]{2,1,0:T(8,128)(2,1)S(1)}, bf16[128,102,128]{2,1,0:T(8,128)(2,1)S(1)}) custom-call(s32[128]{0:T(128)S(1)} %get-tuple-element.46.place_ref, s32[128]{0:T(128)S(1)} %copy-done.5, bf16[128,64,128]{2,1,0:T(8,128)(2,1)S(1)} %copy-done.4, bf16[6,102,64]{2,1,0:T(8,128)(2,1)S(1)} %copy.16.weights_ref), custom_call_target="tpu_custom_call" | custom-call | tf_op jit(solution)/shard_map/partial_sums/pallas_call | solution.py:54
  11.3 1.7 %copy-done = bf16[128,102,128]{2,1,0:T(8,128)(2,1)} copy-done((bf16[128,102,128]{2,1,0:T(8,128)(2,1)}, bf16[128,102,128]{2,1,0:T(8,128)(2,1)S(1)}, u32[]{:S(2)}) %copy-start) | copy-done | bytes 3342360
  13.0 1.8 %copy-done.2 = bf16[128,102,128]{2,1,0:T(8,128)(2,1)} copy-done((bf16[128,102,128]{2,1,0:T(8,128)(2,1)}, bf16[128,102,128]{2,1,0:T(8,128)(2,1)S(1)}, u32[]{:S(2)}) %copy-start.2) | copy-done | bytes 3342360
  14.7 0.1 convert_reduce_fusion
  14.9 0.1 reshape.182
  14.9 0.9 convert_reduce_fusion.1
  15.9 0.7 multiply_add_fusion
  16.6 0.1 select_reduce_fusion.1
  16.7 0.1 reshape.183
  16.8 0.1 pad_add_fusion
  16.8 0.1 broadcast_in_dim.24.notes_ref
  17.0 2.0 %copy-done.1 = bf16[128,102,128]{2,1,0:T(8,128)(2,1)S(1)} copy-done((bf16[128,102,128]{2,1,0:T(8,128)(2,1)S(1)}, bf16[128,102,128]{2,1,0:T(8,128)(2,1)}, u32[]{:S(2)}) %copy-start.1) | copy-done | bytes 3342360
  18.9 2.0 %copy-done.3 = bf16[128,102,128]{2,1,0:T(8,128)(2,1)S(1)} copy-done((bf16[128,102,128]{2,1,0:T(8,128)(2,1)S(1)}, bf16[128,102,128]{2,1,0:T(8,128)(2,1)}, u32[]{:S(2)}) %copy-start.3) | copy-done | bytes 3342360
  20.9 60.1 %reduce_rows.1 = (bf16[20,102,128]{2,1,0:T(8,128)(2,1)S(1)}, s32[16,8,128]{2,1,0:T(8,128)S(1)}) custom-call(s32[16,24,128]{2,1,0:T(8,128)S(1)} %broadcast_in_dim.24.notes_ref, bf16[128,102,128]{2,1,0:T(8,128)(2,1)S(1)} %copy-done.1, bf16[128,102,128]{2,1,0:T(8,128)(2,1)S(1)} %copy-done.3), custom_call_target="tpu_custom_call" | custom-call | tf_op jit(solution)/shard_map/reduce_rows/pallas_call | solution.py:314
  81.0 0.9 divide_reduce_fusion.1
  81.9 0.1 div.69
  82.0 0.1 div.71
  82.1 0.1 rem.224
  82.2 0.6 fusion.4
  82.8 0.1 ne.138
  82.9 0.1 ne.140
  83.1 3.7 %add_convert_fusion = bf16[16,102,128]{2,1,0:T(8,128)(2,1)S(1)} fusion(bf16[20,102,128]{2,1,0:T(8,128)(2,1)S(1)} %get-tuple-element.8, f32[102]{0:T(128)S(1)} %get-tuple-element.44, f32[102]{0:T(128)S(1)} %get-tuple-element.45, f32[102]{0:T(128)S(1)} %get-tuple-element.22, f32[102]{0:T(128)S(1)} %get-tuple-element.23, f32[102]{0:T(128)S(1)} %get-tuple-element.24, ...), kind=kLoop, calls=%fused_computation.25 | loop fusion | flops 15667200 | bytes 3092992 | tf_op jit(solution)/shard_map/convert_element_type | solution.py:452
  86.9 0.3 convolution_bitcast_fusion
  87.2 0.4 select_reduce_fusion
  87.6 0.1 copy.17
  87.7 9.9 %exchange.1 = f32[16,8,128]{2,1,0:T(8,128)S(1)} custom-call(f32[16,8,128]{2,1,0:T(8,128)S(1)} %bitcast.59), custom_call_target="tpu_custom_call" | custom-call | tf_op jit(solution)/shard_map/exchange/pallas_call | solution.py:369
  97.6 0.8 convolution_convert_fusion
  98.4 0.8 copy.18
  (16 shorter events, 0.1 us)
Async XLA Ops:
  2.4 1.6 %copy-start.4 = (bf16[128,64,128]{2,1,0:T(8,128)(2,1)S(1)}, bf16[128,64,128]{2,1,0:T(8,128)(2,1)}, u32[]{:S(2)}) copy-start(bf16[128,64,128]{2,1,0:T(8,128)(2,1)} %pixels_ref.1) | copy-start | bytes 6291460
  4.0 0.7 copy-start.5
  11.3 1.7 %copy-start = (bf16[128,102,128]{2,1,0:T(8,128)(2,1)}, bf16[128,102,128]{2,1,0:T(8,128)(2,1)S(1)}, u32[]{:S(2)}) copy-start(bf16[128,102,128]{2,1,0:T(8,128)(2,1)S(1)} %get-tuple-element.6.keep_ref) | copy-start | bytes 10027012
  13.0 1.8 %copy-start.2 = (bf16[128,102,128]{2,1,0:T(8,128)(2,1)}, bf16[128,102,128]{2,1,0:T(8,128)(2,1)S(1)}, u32[]{:S(2)}) copy-start(bf16[128,102,128]{2,1,0:T(8,128)(2,1)S(1)} %get-tuple-element.7.send_ref) | copy-start | bytes 10027012
  17.0 2.0 %copy-start.1 = (bf16[128,102,128]{2,1,0:T(8,128)(2,1)S(1)}, bf16[128,102,128]{2,1,0:T(8,128)(2,1)}, u32[]{:S(2)}) copy-start(bf16[128,102,128]{2,1,0:T(8,128)(2,1)} %copy-done) | copy-start | bytes 10027012
  18.9 2.0 %copy-start.3 = (bf16[128,102,128]{2,1,0:T(8,128)(2,1)S(1)}, bf16[128,102,128]{2,1,0:T(8,128)(2,1)}, u32[]{:S(2)}) copy-start(bf16[128,102,128]{2,1,0:T(8,128)(2,1)} %copy-done.2) | copy-start | bytes 10027012
  20.9 62.2 %copy-start.6 = (f32[102,25]{0,1:T(8,128)S(1)}, f32[102,25]{0,1:T(8,128)}, u32[]{:S(2)}) copy-start(f32[102,25]{0,1:T(8,128)} %param.15) | copy-start | bytes 30604

commit v3 on v2

--- a/solution.py
+++ b/solution.py
@@ -10,12 +10,18 @@
 TROWS = 16
 F32 = jnp.float32
 BF16 = jnp.bfloat16
-CHUNKS = 4
+CHUNKS = 8
+PART = TROWS // CHUNKS
+SLAB = 4 * PART
+ORDER = (0, 7, 1, 2, 3, 4, 5, 6)
 MESH = pl.DeviceIdType.MESH
 GROUP = 8
 
 
-def partial_sums_kernel(place_ref, band_ref, pixels_ref, weights_ref, keep_ref, send_ref, total):
+def partial_sums_kernel(
+    place_ref, band_ref, pixels_ref, weights_ref, keep_hbm, send_hbm,
+    total, keep_ref, send_ref, out_sem,
+):
     blocks = pixels_ref.shape[0]
     half = total.shape[0] // 2
 
@@ -39,12 +45,22 @@
 
     lax.fori_loop(0, blocks // GROUP, step, 0)
 
-    def emit(i, _):
-        keep_ref[i] = total[i].astype(BF16)
-        send_ref[i] = total[half + i].astype(BF16)
-        return 0
-
-    lax.fori_loop(0, half, emit, 0, unroll=4)
+    copies = []
+    for far in (1, 0):
+        rows = pl.ds(far * half // 2, half // 2)
+        for n, (buffer, out) in enumerate(((send_ref, send_hbm), (keep_ref, keep_hbm))):
+            source = (half if n == 0 else 0) + far * half // 2
+
+            def emit(i, _, buffer=buffer, source=source, far=far):
+                buffer[far * half // 2 + i] = total[source + i].astype(BF16)
+                return 0
+
+            lax.fori_loop(0, half // 2, emit, 0, unroll=4)
+            copy = pltpu.make_async_copy(buffer.at[rows], out.at[rows], out_sem.at[2 * far + n])
+            copy.start()
+            copies.append(copy)
+    for copy in copies:
+        copy.wait()
 
 
 def partial_sums(place, band, pixels, weights, rows):
@@ -55,8 +71,13 @@
         partial_sums_kernel,
         out_shape=[jax.ShapeDtypeStruct((rows // 2, channels, columns), BF16)] * 2,
         in_specs=[smem, smem, vmem, vmem],
-        out_specs=[vmem] * 2,
-        scratch_shapes=[pltpu.VMEM((rows, channels, columns), F32)],
+        out_specs=[pl.BlockSpec(memory_space=pltpu.HBM)] * 2,
+        scratch_shapes=[
+            pltpu.VMEM((rows, channels, columns), F32),
+            pltpu.VMEM((rows // 2, channels, columns), BF16),
+            pltpu.VMEM((rows // 2, channels, columns), BF16),
+            pltpu.SemaphoreType.DMA((4,)),
+        ],
         compiler_params=pltpu.CompilerParams(vmem_limit_bytes=40 * 1024 * 1024),
         name="partial_sums",
     )(place, band, pixels, weights)
@@ -88,9 +109,10 @@
 
 
 def reduce_kernel(
-    notes_ref, keep_ref, send_ref, rows_ref, notes_out_ref,
-    notes_in, from_core, to_x, from_x, plane, chain_out, chain_in, halo_in,
-    note_send, note_recv, core_send, core_recv, x_send, x_recv,
+    notes_ref, keep_hbm, send_ref, psf_ref, mine_ref, cube_ref, rest_ref,
+    notes_in, keep_ref, from_core, to_x, from_x, plane, chain_out, chain_in, halo_in, rows_ref,
+    taps, picked, window_out, window_in,
+    note_send, note_recv, window_send, window_recv, keep_sem, core_send, core_recv, x_send, x_recv,
     chain_send, chain_recv, halo_send, halo_recv,
 ):
     count = 16
@@ -98,8 +120,8 @@
     z, x, c = me // 4, (me // 2) % 2, me % 2
     other_core = me + 1 - 2 * c
     other_x = me + 2 - 4 * x
-    part = TROWS // CHUNKS
-    size = 4 * part
+    part, size = PART, SLAB
+    channels, columns = cube_ref.shape[1], cube_ref.shape[2]
 
     def remote(src, dst, send_sem, recv_sem, there):
         return pltpu.make_async_remote_copy(
@@ -129,6 +151,15 @@
     def note(k):
         return exchange_copy(k, me, count, notes_ref, notes_in, note_send, note_recv)
 
+    def window(k):
+        return exchange_copy(k, me, count, window_out, window_in, window_send, window_recv)
+
+    def keep_copy(far):
+        rows = pl.ds(far * CHUNKS * size, CHUNKS * size)
+        return pltpu.make_async_copy(keep_hbm.at[rows], keep_ref.at[rows], keep_sem.at[far])
+
+    keep_copy(1).start()
+    keep_copy(0).start()
     greet_all(me, count)
     for k in range(CHUNKS):
         core_copy(1, k).start()
@@ -139,6 +170,7 @@
 
     lax.fori_loop(1, count, send_note, 0)
 
+    keep_copy(1).wait()
     for k in range(CHUNKS):
         core_copy(1, k).wait_recv()
 
@@ -160,7 +192,16 @@
 
     lax.fori_loop(1, count, wait_note, 0)
     notes_in[me] = notes_ref[me]
-    notes_out_ref[...] = notes_in[:, TROWS:, :]
+    keep_copy(0).wait()
+    words = notes_in[:, TROWS:, :].reshape(-1, 128)
+    slot_shift = words & 63
+    slot_col = (words >> 6) & 127
+    slot_row = words >> 13
+    lane = lax.broadcasted_iota(jnp.int32, words.shape, 1)
+    on_column = slot_col == lane
+    picked[...] = jnp.zeros(picked.shape, F32)
+    for tap in range(KW * KW):
+        taps[tap] = jnp.broadcast_to(psf_ref[:, tap : tap + 1], (channels, columns))
     counts = jnp.maximum(jnp.sum(notes_in[:, :TROWS, :], axis=0).astype(F32), 1.0)
 
     def sends(way, dist):
@@ -225,7 +266,7 @@
             value = plane[k * size + z * part + i].astype(F32)
             value = value + jnp.where(up_on, chain_in[up_at + i].astype(F32), 0.0)
             value = value + jnp.where(down_on, chain_in[down_at + i].astype(F32), 0.0)
-            row = k * part + i
+            row = ORDER[k] * part + i
             rows_ref[2 + row] = (value / counts[row : row + 1, :]).astype(BF16)
 
     def halo_copy(way):
@@ -236,51 +277,99 @@
             halo_recv.at[way], there,
         )
 
+    def match_row(y, _):
+        radius = KW // 2
+        near = [rows_ref[y + dy].astype(F32) for dy in range(KW)]
+        at = lax.broadcasted_iota(jnp.int32, (channels, columns), 1)
+        total = None
+        for dx in range(KW):
+            term = taps[dx] * near[0]
+            for dy in range(1, KW):
+                term = term + taps[dy * KW + dx] * near[dy]
+            offset = dx - radius
+            if offset != 0:
+                term = pltpu.roll(term, (-offset) % columns, 1)
+                valid = at < columns - offset if offset > 0 else at >= -offset
+                term = jnp.where(valid, term, 0.0)
+            total = term if total is None else total + term
+        matched = total.astype(BF16)
+        cube_ref[y] = matched
+        chosen = jnp.where(jnp.logical_and(on_column, slot_row == y), 1.0, 0.0).astype(BF16)
+        picked[:, :channels] += lax.dot_general(
+            chosen, matched, (((1,), (1,)), ((), ())), preferred_element_type=F32
+        )
+        return 0
+
+    def take_halo():
+        @pl.when(me <= count - 2)
+        def _():
+            halo_copy(0).wait_recv()
+            for i in range(2):
+                rows_ref[TROWS + 2 + i] = halo_in[i]
+
+        @pl.when(me >= 1)
+        def _():
+            halo_copy(1).wait_recv()
+            for i in range(2):
+                rows_ref[i] = halo_in[2 + i]
+
     def done(k):
         finish(k)
         if k == 0:
             @pl.when(me >= 1)
             def _():
                 halo_copy(0).start()
-        if k == CHUNKS - 1:
+        if k == 1:
             @pl.when(me <= count - 2)
             def _():
                 halo_copy(1).start()
-
-    for k in range(CHUNKS):
-        core_copy(0, k).wait_recv()
-        x_copy(k).wait_recv()
-
-        def add_plane(i, _, k=k):
-            at = k * size + i
-            plane[at] = (
-                keep_ref[at].astype(F32) + from_core[at].astype(F32) + from_x[at].astype(F32)
-            ).astype(BF16)
-            return 0
-
-        lax.fori_loop(0, size, add_plane, 0)
-        hop(k, 3)
-        if k > 0:
-            done(k - 1)
-        hop(k, 2)
-        hop(k, 1)
-    done(CHUNKS - 1)
+        if k == 4:
+            take_halo()
+            lax.fori_loop(0, 2, match_row, 0)
+        if k >= 3:
+            lax.fori_loop(2 * k - 4, 2 * k - 2 if k < CHUNKS - 1 else TROWS, match_row, 0)
 
     for i in range(2):
         rows_ref[i] = jnp.zeros(rows_ref.shape[1:], BF16)
         rows_ref[TROWS + 2 + i] = jnp.zeros(rows_ref.shape[1:], BF16)
 
-    @pl.when(me <= count - 2)
-    def _():
-        halo_copy(0).wait_recv()
-        for i in range(2):
-            rows_ref[TROWS + 2 + i] = halo_in[i]
-
-    @pl.when(me >= 1)
-    def _():
-        halo_copy(1).wait_recv()
-        for i in range(2):
-            rows_ref[i] = halo_in[2 + i]
+    for t in range(CHUNKS + 3):
+        if t < CHUNKS:
+            core_copy(0, t).wait_recv()
+            x_copy(t).wait_recv()
+
+            def add_plane(i, _, t=t):
+                at = t * size + i
+                plane[at] = (
+                    keep_ref[at].astype(F32) + from_core[at].astype(F32) + from_x[at].astype(F32)
+                ).astype(BF16)
+                return 0
+
+            lax.fori_loop(0, size, add_plane, 0)
+            hop(t, 3)
+        if 0 <= t - 1 < CHUNKS:
+            hop(t - 1, 2)
+        if 0 <= t - 2 < CHUNKS:
+            hop(t - 2, 1)
+        if t >= 3:
+            done(t - 3)
+
+    chosen_window = picked[...]
+    for bit in range(6):
+        moved = pltpu.roll(chosen_window, 128 - 2**bit, 1)
+        chosen_window = jnp.where((slot_shift >> bit) & 1 == 1, moved, chosen_window)
+    window_out[...] = chosen_window.reshape(window_out.shape)
+
+    def send_window(k, _):
+        window(k).start()
+        return 0
+
+    def take_window(k, _):
+        window(k).wait()
+        return 0
+
+    lax.fori_loop(1, count, send_window, 0)
+    window_in[me] = window_out[me]
 
     @pl.when(me >= 1)
     def _():
@@ -304,23 +393,29 @@
                 @pl.when(sends(way, dist))
                 def _(way=way, k=k, dist=dist):
                     chain_copy(way, k, dist).wait_send()
-
-
-def reduce_rows_and_notes(notes, keep, send):
+    lax.fori_loop(1, count, take_window, 0)
+    landed = window_in[...].reshape(-1, 128).astype(BF16)
+    rest = jnp.dot(mine_ref[...], landed, preferred_element_type=F32)
+    rest_ref[...] = rest[:, :NW].astype(BF16)
+
+
+def reduce_and_match(notes, keep, send, psf_kernel, mine):
     tail = keep.shape[1:]
     vmem = pl.BlockSpec(memory_space=pltpu.VMEM)
-    part = TROWS // CHUNKS
+    hbm = pl.BlockSpec(memory_space=pltpu.HBM)
     dma = pltpu.SemaphoreType.DMA
+    slots = mine.shape[1]
     return pl.pallas_call(
         reduce_kernel,
         out_shape=[
-            jax.ShapeDtypeStruct((TROWS + 4,) + tail, BF16),
-            jax.ShapeDtypeStruct((16, notes.shape[1] - TROWS, 128), jnp.int32),
+            jax.ShapeDtypeStruct((TROWS,) + tail, BF16),
+            jax.ShapeDtypeStruct((mine.shape[0], NW), BF16),
         ],
-        in_specs=[vmem] * 3,
+        in_specs=[vmem, hbm, hbm, vmem, vmem],
         out_specs=[vmem] * 2,
         scratch_shapes=[
             pltpu.VMEM(notes.shape, jnp.int32),
+            pltpu.VMEM((8 * TROWS,) + tail, BF16),
             pltpu.VMEM((8 * TROWS,) + tail, BF16),
             pltpu.VMEM((4 * TROWS,) + tail, BF16),
             pltpu.VMEM((4 * TROWS,) + tail, BF16),
@@ -328,73 +423,36 @@
             pltpu.VMEM((6 * TROWS,) + tail, BF16),
             pltpu.VMEM((6 * TROWS,) + tail, BF16),
             pltpu.VMEM((4,) + tail, BF16),
-            dma((16,)), dma((16,)),
+            pltpu.VMEM((TROWS + 4,) + tail, BF16),
+            pltpu.VMEM((KW * KW,) + tail, F32),
+            pltpu.VMEM((slots, 128), F32),
+            pltpu.VMEM((16, slots // 16, 128), F32),
+            pltpu.VMEM((16, slots // 16, 128), F32),
+            dma((16,)), dma((16,)), dma((16,)), dma((16,)), dma((2,)),
             dma((2 * CHUNKS,)), dma((2 * CHUNKS,)),
             dma((CHUNKS,)), dma((CHUNKS,)),
             dma((6 * CHUNKS,)), dma((6 * CHUNKS,)),
             dma((2,)), dma((2,)),
         ],
         compiler_params=pltpu.CompilerParams(
-            collective_id=0, has_side_effects=True, vmem_limit_bytes=40 * 1024 * 1024
+            collective_id=0, has_side_effects=True, vmem_limit_bytes=48 * 1024 * 1024
         ),
-        name="reduce_rows",
-    )(notes, keep, send)
-
-
-def exchange_kernel(out_ref, in_ref, landed, send_sem, recv_sem):
-    count = out_ref.shape[0]
-    me = lax.axis_index("tile")
-
-    def copy(k):
-        return exchange_copy(k, me, count, out_ref, landed, send_sem, recv_sem)
-
-    greet_all(me, count)
-
-    def start(k, _):
-        copy(k).start()
-        return 0
-
-    def wait(k, _):
-        copy(k).wait()
-        return 0
-
-    lax.fori_loop(1, count, start, 0)
-    landed[me] = out_ref[me]
-    lax.fori_loop(1, count, wait, 0)
-    in_ref[...] = landed[...]
-
-
-def exchange(values):
-    vmem = pl.BlockSpec(memory_space=pltpu.VMEM)
-    return pl.pallas_call(
-        exchange_kernel,
-        out_shape=jax.ShapeDtypeStruct(values.shape, values.dtype),
-        in_specs=[vmem],
-        out_specs=vmem,
-        scratch_shapes=[
-            pltpu.VMEM(values.shape, values.dtype),
-            pltpu.SemaphoreType.DMA((values.shape[0],)),
-            pltpu.SemaphoreType.DMA((values.shape[0],)),
-        ],
-        compiler_params=pltpu.CompilerParams(
-            collective_id=1, has_side_effects=True, vmem_limit_bytes=40 * 1024 * 1024
-        ),
-        name="exchange",
-    )(values)
-
-
-def averaged_rows(pixels, band, tile, row, weights, counts_out, words_out):
+        name="reduce_and_match",
+    )(notes, keep, send, psf_kernel, mine)
+
+
+def small_body(pixels, band, tile, row, weights, psf_kernel, counts_out, words_out, mine):
     me = lax.axis_index("tile")
     x, c = (me // 2) % 2, me % 2
     dest_z, dest_x, dest_c = tile // 4, (tile // 2) % 2, tile % 2
     far_x, far_c = (dest_x + x) % 2, (dest_c + c) % 2
-    part = TROWS // CHUNKS
-    place = (((far_c * 2 + far_x) * CHUNKS + row // part) * 4 + dest_z) * part + row % part
+    pair = row // PART
+    chunk = jnp.where(pair == 0, 0, jnp.where(pair == CHUNKS - 1, 1, pair + 1))
+    place = (((far_c * 2 + far_x) * CHUNKS + chunk) * 4 + dest_z) * PART + row % PART
     keep, send = partial_sums(place, band, pixels, weights, 16 * TROWS)
     notes = jnp.concatenate([counts_out, words_out], axis=1)
     notes = jnp.broadcast_to(notes[:, :, None], notes.shape + (128,))
-    rows, notes = reduce_rows_and_notes(notes, keep, send)
-    return rows, notes[:, :, 0].reshape(-1)
+    return reduce_and_match(notes, keep, send, psf_kernel, mine)
 
 
 def averaged_rows_any(pixels, band, tile, row, weights, counts_out, words_out):
@@ -468,7 +526,7 @@
     channels, columns = band_weights.shape[1], exposure_pixels.shape[2]
     gal_here = gal_tile.shape[0]
     depth = min(8, gal_here)
-    span = channels - NW + 1
+    span = 64
     tile_range = jnp.arange(tile_count, dtype=jnp.int32)
     row_range = jnp.arange(TROWS, dtype=jnp.int32)
 
@@ -481,10 +539,16 @@
     words_out = jnp.sum(
         jnp.where(place[None, :] == slot_range[:, None], word[None, :], 0), axis=1
     )
-    small = tile_count == 16
-    coadded, words = (averaged_rows if small else averaged_rows_any)(
-        exposure_pixels, block_band, block_tile, block_row, band_weights,
-        counts_out.reshape(tile_count, TROWS), words_out.reshape(tile_count, depth),
+    mine = (place[:, None] == slot_range[None, :]).astype(BF16)
+    counts_out = counts_out.reshape(tile_count, TROWS)
+    words_out = words_out.reshape(tile_count, depth)
+    if tile_count == 16:
+        return small_body(
+            exposure_pixels, block_band, block_tile, block_row, band_weights, psf_kernel,
+            counts_out, words_out, mine,
+        )
+    coadded, words = averaged_rows_any(
+        exposure_pixels, block_band, block_tile, block_row, band_weights, counts_out, words_out
     )
     slot_shift = words % span
     slot_col = (words // span) % columns
@@ -503,13 +567,7 @@
     channel_range = jnp.arange(channels, dtype=jnp.int32)
     inside = channel_range[None, :, None] == (slot_shift[None, :] + window[:, None])[:, None, :]
     values = jnp.sum(jnp.where(inside, spectra[None], 0.0), axis=1).T.astype(BF16)
-    if small:
-        values = jnp.pad(values, ((0, 0), (0, 128 - NW))).astype(F32)
-        returned = exchange(values.reshape(tile_count, depth, 128))
-        returned = returned.reshape(-1, 128)[:, :NW].astype(BF16)
-    else:
-        returned = lax.all_to_all(values, "tile", split_axis=0, concat_axis=0, tiled=True)
-    mine = (place[:, None] == slot_range[None, :]).astype(BF16)
+    returned = lax.all_to_all(values, "tile", split_axis=0, concat_axis=0, tiled=True)
     rest_spectra = jnp.dot(mine, returned, preferred_element_type=F32).astype(BF16)
     return matched_cube, rest_spectra
 

time: 99.5 us -> 86.1 us (0.87)
  other arithmetic: 8.35 us -> 2.7 us
  local copies, waits for them, and re-layouts: 12.4 us -> 7.54 us
  Pallas kernels: 76.5 us -> 74.9 us
  matrix products: 1.09 us -> 0 us
    unnamed x16 -> x9, local copies, waits for them, and re-layouts: 11.5 us -> 6.46 us
    convert_element_type x1, other arithmetic: 3.74 us -> 0.07 us  [body(): mine = (place[:, None] == slot_range[None, :]).astype(BF16)]
    pallas_call x2 -> x1, Pallas kernels: 70 us -> 66.9 us  [reduce_and_match(): pl.pallas_call(reduce_kernel, out_shape=[jax.ShapeDtypeStruct((TROWS,) +...]
    pallas_call x1, Pallas kernels: 6.57 us -> 7.96 us  [partial_sums(): pl.pallas_call(partial_sums_kernel, out_shape=[jax.ShapeDtypeStruct((rows...]
    dot_general x2 -> x0, matrix products: 1.09 us -> none  [the longest x1 0.8 us: body(): jnp.dot(mine, returned, preferred_element_type=F32).astype(BF16)]
where the time goes in v3:
time: 86.1 us; the launch traced here: 85.8 us
  Pallas kernels  74.9 us (87%)
  local copies, waits for them, and re-layouts  7.54 us (9%)
  other arithmetic  2.7 us (3%)
    pallas_call x1, Pallas kernels, reduce_and_match(): pl.pallas_call(reduce_kernel, out_shape=[jax.ShapeDtypeStruct((TROWS,) +...  66.9 us
    pallas_call x1, Pallas kernels, partial_sums(): pl.pallas_call(partial_sums_kernel, out_shape=[jax.ShapeDtypeStruct((rows...  7.96 us
    unnamed x9, local copies, waits for them, and re-layouts  6.46 us

profile of v3, /device:TPU:0, one launch (start us, length us, event | category | flops | bytes accessed | tf_op | source)
XLA Modules:
  0.0 85.8 jit_solution(55875452211197351)
XLA Ops:
  0.7 0.7 fusion.3
  1.4 0.9 %convert_reduce_fusion.1 = s32[64]{0:T(128)S(1)} fusion(s32[64]{0:T(128)} %param.16), kind=kLoop, calls=%fused_computation.5 | loop fusion | flops 20416 | bytes 512 | tf_op jit(solution)/shard_map/reduce_sum | solution.py:489
  2.3 0.7 multiply_add_fusion
  3.0 0.1 select_reduce_fusion
  3.1 0.1 convert_reduce_fusion
  3.2 0.1 reshape.17
  3.3 0.1 reshape.18
  3.4 0.1 pad_add_fusion
  3.5 0.1 fusion.1.mine_ref
  3.5 0.8 copy.19.psf_ref
  4.4 1.1 %copy.18.weights_ref = bf16[6,102,64]{2,1,0:T(8,128)(2,1)S(1)} copy(bf16[6,102,64]{1,2,0:T(8,128)(2,1)} %param.14) | data formatting | bytes 156672 | tf_op args[4]
  5.4 0.1 broadcast_in_dim.18.notes_ref
  5.5 0.0 copy-start.1
  5.6 1.6 %copy-done.1 = bf16[128,64,128]{2,1,0:T(8,128)(2,1)S(1)} copy-done((bf16[128,64,128]{2,1,0:T(8,128)(2,1)S(1)}, bf16[128,64,128]{2,1,0:T(8,128)(2,1)}, u32[]{:S(2)}) %copy-start.1) | copy-done | bytes 2097176
  7.1 0.0 copy-start.2
  7.1 0.7 copy-done.2
  7.8 8.0 %partial_sums.1 = (bf16[128,102,128]{2,1,0:T(8,128)(2,1)S(1)}, bf16[128,102,128]{2,1,0:T(8,128)(2,1)S(1)}) custom-call(s32[128]{0:T(128)S(1)} %get-tuple-element.12.place_ref, s32[128]{0:T(128)S(1)} %copy-done.2, bf16[128,64,128]{2,1,0:T(8,128)(2,1)S(1)} %copy-done.1, bf16[6,102,64]{2,1,0:T(8,128)(2,1)S(1)} %copy.18.weights_ref), custom_call_target="tpu_custom_call" | custom-call | tf_op jit(solution)/shard_map/partial_sums/pallas_call | solution.py:70
  15.8 0.0 copy-start
  15.8 1.7 %copy-done = bf16[128,102,128]{2,1,0:T(8,128)(2,1)} copy-done((bf16[128,102,128]{2,1,0:T(8,128)(2,1)}, bf16[128,102,128]{2,1,0:T(8,128)(2,1)S(1)}, u32[]{:S(2)}) %copy-start) | copy-done | bytes 3342360
  17.5 66.9 %reduce_and_match.1 = (bf16[16,102,128]{2,1,0:T(8,128)(2,1)S(1)}, bf16[64,64]{1,0:T(8,128)(2,1)S(1)}) custom-call(s32[16,24,128]{2,1,0:T(8,128)S(1)} %broadcast_in_dim.18.notes_ref, bf16[128,102,128]{2,1,0:T(8,128)(2,1)S(1)} %get-tuple-element.4.keep_hbm, bf16[128,102,128]{2,1,0:T(8,128)(2,1)} %copy-done, f32[102,25]{1,0:T(8,128)S(1)} %copy.19.psf_ref, ...), custom_call_target="tpu_custom_call" | custom-call | tf_op jit(solution)/shard_map/reduce_and_match/pallas_call | solution.py:408
  84.4 0.8 copy.20
  85.2 0.6 copy.22
Async XLA Ops:
  5.5 1.6 %copy-start.1 = (bf16[128,64,128]{2,1,0:T(8,128)(2,1)S(1)}, bf16[128,64,128]{2,1,0:T(8,128)(2,1)}, u32[]{:S(2)}) copy-start(bf16[128,64,128]{2,1,0:T(8,128)(2,1)} %pixels_ref.1) | copy-start | bytes 6291460
  7.1 0.7 copy-start.2
  15.8 1.7 %copy-start = (bf16[128,102,128]{2,1,0:T(8,128)(2,1)}, bf16[128,102,128]{2,1,0:T(8,128)(2,1)S(1)}, u32[]{:S(2)}) copy-start(bf16[128,102,128]{2,1,0:T(8,128)(2,1)S(1)} %get-tuple-element.5.send_ref) | copy-start | bytes 10027012

commit v4 on v3

--- a/solution.py
+++ b/solution.py
@@ -19,9 +19,13 @@
 
 
 def partial_sums_kernel(
-    place_ref, band_ref, pixels_ref, weights_ref, keep_hbm, send_hbm,
-    total, keep_ref, send_ref, out_sem,
+    place_ref, band_ref, pixels_hbm, weights_t_ref, keep_hbm, send_hbm,
+    total, pixels_ref, weights_ref, keep_ref, send_ref, in_sem, out_sem,
 ):
+    load = pltpu.make_async_copy(pixels_hbm, pixels_ref, in_sem)
+    load.start()
+    for band in range(weights_ref.shape[0]):
+        weights_ref[band] = weights_t_ref[band].astype(F32).T.astype(BF16)
     blocks = pixels_ref.shape[0]
     half = total.shape[0] // 2
 
@@ -30,6 +34,7 @@
         return 0
 
     lax.fori_loop(0, total.shape[0], clear, 0, unroll=4)
+    load.wait()
 
     def step(i, _):
         spectra = []
@@ -70,17 +75,20 @@
     return pl.pallas_call(
         partial_sums_kernel,
         out_shape=[jax.ShapeDtypeStruct((rows // 2, channels, columns), BF16)] * 2,
-        in_specs=[smem, smem, vmem, vmem],
-        out_specs=[pl.BlockSpec(memory_space=pltpu.HBM)] * 2,
+        in_specs=[smem, smem, pl.BlockSpec(memory_space=pl.ANY), vmem],
+        out_specs=[pl.BlockSpec(memory_space=pl.ANY)] * 2,
         scratch_shapes=[
             pltpu.VMEM((rows, channels, columns), F32),
+            pltpu.VMEM(pixels.shape, BF16),
+            pltpu.VMEM(weights.shape, BF16),
             pltpu.VMEM((rows // 2, channels, columns), BF16),
             pltpu.VMEM((rows // 2, channels, columns), BF16),
+            pltpu.SemaphoreType.DMA,
             pltpu.SemaphoreType.DMA((4,)),
         ],
-        compiler_params=pltpu.CompilerParams(vmem_limit_bytes=40 * 1024 * 1024),
+        compiler_params=pltpu.CompilerParams(vmem_limit_bytes=28 * 1024 * 1024),
         name="partial_sums",
-    )(place, band, pixels, weights)
+    )(place, band, pixels, jnp.swapaxes(weights, 1, 2))
 
 
 def greet_all(me, count):
@@ -161,7 +169,7 @@
     keep_copy(1).start()
     keep_copy(0).start()
     greet_all(me, count)
-    for k in range(CHUNKS):
+    for k in range(3):
         core_copy(1, k).start()
 
     def send_note(k, _):
@@ -170,21 +178,24 @@
 
     lax.fori_loop(1, count, send_note, 0)
 
-    keep_copy(1).wait()
-    for k in range(CHUNKS):
+    def cross(k):
         core_copy(1, k).wait_recv()
 
-        def add_x(i, _, k=k):
+        def add_x(i, _):
             at = (CHUNKS + k) * size + i
             to_x[k * size + i] = (
                 keep_ref[at].astype(F32) + from_core[at].astype(F32)
             ).astype(BF16)
             return 0
 
-        lax.fori_loop(0, size, add_x, 0)
+        lax.fori_loop(0, size, add_x, 0, unroll=2)
         x_copy(k).start()
-    for k in range(CHUNKS):
-        core_copy(0, k).start()
+
+    keep_copy(1).wait()
+    cross(0)
+    core_copy(0, 0).start()
+    cross(1)
+    core_copy(0, 1).start()
 
     def wait_note(k, total):
         note(k).wait_recv()
@@ -200,8 +211,9 @@
     lane = lax.broadcasted_iota(jnp.int32, words.shape, 1)
     on_column = slot_col == lane
     picked[...] = jnp.zeros(picked.shape, F32)
+    psf = psf_ref[...].T
     for tap in range(KW * KW):
-        taps[tap] = jnp.broadcast_to(psf_ref[:, tap : tap + 1], (channels, columns))
+        taps[tap] = jnp.broadcast_to(psf[:, tap : tap + 1], (channels, columns))
     counts = jnp.maximum(jnp.sum(notes_in[:, :TROWS, :], axis=0).astype(F32), 1.0)
 
     def sends(way, dist):
@@ -335,8 +347,13 @@
 
     for t in range(CHUNKS + 3):
         if t < CHUNKS:
+            x_copy(t).wait_recv()
+            if t + 2 < CHUNKS:
+                cross(t + 2)
+                core_copy(0, t + 2).start()
+            if t + 3 < CHUNKS:
+                core_copy(1, t + 3).start()
             core_copy(0, t).wait_recv()
-            x_copy(t).wait_recv()
 
             def add_plane(i, _, t=t):
                 at = t * size + i
@@ -345,7 +362,7 @@
                 ).astype(BF16)
                 return 0
 
-            lax.fori_loop(0, size, add_plane, 0)
+            lax.fori_loop(0, size, add_plane, 0, unroll=2)
             hop(t, 3)
         if 0 <= t - 1 < CHUNKS:
             hop(t - 1, 2)
@@ -402,7 +419,7 @@
 def reduce_and_match(notes, keep, send, psf_kernel, mine):
     tail = keep.shape[1:]
     vmem = pl.BlockSpec(memory_space=pltpu.VMEM)
-    hbm = pl.BlockSpec(memory_space=pltpu.HBM)
+    hbm = pl.BlockSpec(memory_space=pl.ANY)
     dma = pltpu.SemaphoreType.DMA
     slots = mine.shape[1]
     return pl.pallas_call(
@@ -435,10 +452,10 @@
             dma((2,)), dma((2,)),
         ],
         compiler_params=pltpu.CompilerParams(
-            collective_id=0, has_side_effects=True, vmem_limit_bytes=48 * 1024 * 1024
+            collective_id=0, has_side_effects=True, vmem_limit_bytes=28 * 1024 * 1024
         ),
         name="reduce_and_match",
-    )(notes, keep, send, psf_kernel, mine)
+    )(notes, keep, send, psf_kernel.T, mine)
 
 
 def small_body(pixels, band, tile, row, weights, psf_kernel, counts_out, words_out, mine):

time: 86.1 us -> 84.6 us (0.983)
  local copies, waits for them, and re-layouts: 7.54 us -> 5.54 us
    unnamed x9, local copies, waits for them, and re-layouts: 6.46 us -> 4.45 us
where the time goes in v4:
time: 84.6 us; the launch traced here: 84.3 us
  Pallas kernels  75.4 us (89%)
  local copies, waits for them, and re-layouts  5.54 us (7%)
  other arithmetic  2.7 us (3%)
    pallas_call x1, Pallas kernels, reduce_and_match(): pl.pallas_call(reduce_kernel, out_shape=[jax.ShapeDtypeStruct((TROWS,) +...  67.2 us
    pallas_call x1, Pallas kernels, partial_sums(): pl.pallas_call(partial_sums_kernel, out_shape=[jax.ShapeDtypeStruct((rows...  8.19 us
    unnamed x9, local copies, waits for them, and re-layouts  4.45 us

profile of v4, /device:TPU:0, one launch (start us, length us, event | category | flops | bytes accessed | tf_op | source)
XLA Modules:
  0.0 84.3 jit_solution(11699629621926954051)
XLA Ops:
  0.7 0.7 fusion.3
  1.4 0.9 %convert_reduce_fusion.1 = s32[64]{0:T(128)S(1)} fusion(s32[64]{0:T(128)} %param.16), kind=kLoop, calls=%fused_computation.5 | loop fusion | flops 20416 | bytes 512 | tf_op jit(solution)/shard_map/reduce_sum | solution.py:506
  2.3 0.7 multiply_add_fusion
  3.0 0.1 select_reduce_fusion
  3.1 0.1 convert_reduce_fusion
  3.2 0.1 reshape.17
  3.3 0.1 reshape.18
  3.4 0.1 pad_add_fusion
  3.5 0.1 fusion.1.mine_ref
  3.5 0.1 broadcast_in_dim.18.notes_ref
  3.7 0.0 copy-start
  3.7 1.6 %copy-done = bf16[128,64,128]{2,1,0:T(8,128)(2,1)S(1)} copy-done((bf16[128,64,128]{2,1,0:T(8,128)(2,1)S(1)}, bf16[128,64,128]{2,1,0:T(8,128)(2,1)}, u32[]{:S(2)}) %copy-start) | copy-done | bytes 2097176
  5.3 0.0 copy-start.1
  5.3 0.9 %copy-done.1 = bf16[6,102,64]{1,2,0:T(8,128)(2,1)S(1)} copy-done((bf16[6,102,64]{1,2,0:T(8,128)(2,1)S(1)}, bf16[6,102,64]{1,2,0:T(8,128)(2,1)}, u32[]{:S(2)}) %copy-start.1) | copy-done | bytes 78360
  6.2 0.0 copy-start.3
  6.2 0.7 copy-done.3
  6.8 8.2 %partial_sums.1 = (bf16[128,102,128]{2,1,0:T(8,128)(2,1)S(1)}, bf16[128,102,128]{2,1,0:T(8,128)(2,1)S(1)}) custom-call(s32[128]{0:T(128)S(1)} %get-tuple-element.12.place_ref, s32[128]{0:T(128)S(1)} %copy-done.3, bf16[128,64,128]{2,1,0:T(8,128)(2,1)S(1)} %copy-done, bf16[6,64,102]{2,1,0:T(8,128)(2,1)S(1)} %bitcast.2), custom_call_target="tpu_custom_call" | custom-call | tf_op jit(solution)/shard_map/partial_sums/pallas_call | solution.py:75
  15.0 0.0 copy-start.2
  15.0 0.7 copy-done.2
  15.7 67.2 %reduce_and_match.1 = (bf16[16,102,128]{2,1,0:T(8,128)(2,1)S(1)}, bf16[64,64]{1,0:T(8,128)(2,1)S(1)}) custom-call(s32[16,24,128]{2,1,0:T(8,128)S(1)} %broadcast_in_dim.18.notes_ref, bf16[128,102,128]{2,1,0:T(8,128)(2,1)S(1)} %get-tuple-element.4.keep_hbm, bf16[128,102,128]{2,1,0:T(8,128)(2,1)S(1)} %get-tuple-element.5.send_ref, f32[25,102]{1,0:T(8,128)S(1)} %bitcast.3, ...), custom_call_target="tpu_custom_call" | custom-call | tf_op jit(solution)/shard_map/reduce_and_match/pallas_call | solution.py:425
  82.9 0.8 copy.14
  83.7 0.6 copy.16
Async XLA Ops:
  3.7 1.6 %copy-start = (bf16[128,64,128]{2,1,0:T(8,128)(2,1)S(1)}, bf16[128,64,128]{2,1,0:T(8,128)(2,1)}, u32[]{:S(2)}) copy-start(bf16[128,64,128]{2,1,0:T(8,128)(2,1)} %pixels_hbm.1) | copy-start | bytes 6291460
  5.3 0.9 %copy-start.1 = (bf16[6,102,64]{1,2,0:T(8,128)(2,1)S(1)}, bf16[6,102,64]{1,2,0:T(8,128)(2,1)}, u32[]{:S(2)}) copy-start(bf16[6,102,64]{1,2,0:T(8,128)(2,1)} %param.14) | copy-start | bytes 235012
  6.2 0.7 copy-start.3
  15.0 0.7 copy-start.2

commit v5 on v4

--- a/solution.py
+++ b/solution.py
@@ -13,6 +13,11 @@
 CHUNKS = 8
 PART = TROWS // CHUNKS
 SLAB = 4 * PART
+
+
+def padded_channels(channels):
+    return -(-channels // 8) * 8
+
 ORDER = (0, 7, 1, 2, 3, 4, 5, 6)
 MESH = pl.DeviceIdType.MESH
 GROUP = 8
@@ -24,8 +29,11 @@
 ):
     load = pltpu.make_async_copy(pixels_hbm, pixels_ref, in_sem)
     load.start()
+    weights_ref[...] = jnp.zeros(weights_ref.shape, BF16)
     for band in range(weights_ref.shape[0]):
-        weights_ref[band] = weights_t_ref[band].astype(F32).T.astype(BF16)
+        weights_ref[band, : weights_t_ref.shape[2]] = (
+            weights_t_ref[band].astype(F32).T.astype(BF16)
+        )
     blocks = pixels_ref.shape[0]
     half = total.shape[0] // 2
 
@@ -69,7 +77,7 @@
 
 
 def partial_sums(place, band, pixels, weights, rows):
-    channels, columns = weights.shape[1], pixels.shape[2]
+    channels, columns = padded_channels(weights.shape[1]), pixels.shape[2]
     smem = pl.BlockSpec(memory_space=pltpu.SMEM)
     vmem = pl.BlockSpec(memory_space=pltpu.VMEM)
     return pl.pallas_call(
@@ -80,7 +88,7 @@
         scratch_shapes=[
             pltpu.VMEM((rows, channels, columns), F32),
             pltpu.VMEM(pixels.shape, BF16),
-            pltpu.VMEM(weights.shape, BF16),
+            pltpu.VMEM((weights.shape[0], channels, weights.shape[2]), BF16),
             pltpu.VMEM((rows // 2, channels, columns), BF16),
             pltpu.VMEM((rows // 2, channels, columns), BF16),
             pltpu.SemaphoreType.DMA,
@@ -129,7 +137,8 @@
     other_core = me + 1 - 2 * c
     other_x = me + 2 - 4 * x
     part, size = PART, SLAB
-    channels, columns = cube_ref.shape[1], cube_ref.shape[2]
+    channels, columns = rows_ref.shape[1], rows_ref.shape[2]
+    used = cube_ref.shape[1]
 
     def remote(src, dst, send_sem, recv_sem, there):
         return pltpu.make_async_remote_copy(
@@ -212,8 +221,9 @@
     on_column = slot_col == lane
     picked[...] = jnp.zeros(picked.shape, F32)
     psf = psf_ref[...].T
+    taps[...] = jnp.zeros(taps.shape, F32)
     for tap in range(KW * KW):
-        taps[tap] = jnp.broadcast_to(psf[:, tap : tap + 1], (channels, columns))
+        taps[tap, :used] = jnp.broadcast_to(psf[:, tap : tap + 1], (used, columns))
     counts = jnp.maximum(jnp.sum(notes_in[:, :TROWS, :], axis=0).astype(F32), 1.0)
 
     def sends(way, dist):
@@ -305,7 +315,7 @@
                 term = jnp.where(valid, term, 0.0)
             total = term if total is None else total + term
         matched = total.astype(BF16)
-        cube_ref[y] = matched
+        cube_ref[y] = matched[:used]
         chosen = jnp.where(jnp.logical_and(on_column, slot_row == y), 1.0, 0.0).astype(BF16)
         picked[:, :channels] += lax.dot_general(
             chosen, matched, (((1,), (1,)), ((), ())), preferred_element_type=F32
@@ -416,7 +426,7 @@
     rest_ref[...] = rest[:, :NW].astype(BF16)
 
 
-def reduce_and_match(notes, keep, send, psf_kernel, mine):
+def reduce_and_match(notes, keep, send, psf_t, mine):
     tail = keep.shape[1:]
     vmem = pl.BlockSpec(memory_space=pltpu.VMEM)
     hbm = pl.BlockSpec(memory_space=pl.ANY)
@@ -425,7 +435,7 @@
     return pl.pallas_call(
         reduce_kernel,
         out_shape=[
-            jax.ShapeDtypeStruct((TROWS,) + tail, BF16),
+            jax.ShapeDtypeStruct((TROWS, psf_t.shape[1], tail[1]), BF16),
             jax.ShapeDtypeStruct((mine.shape[0], NW), BF16),
         ],
         in_specs=[vmem, hbm, hbm, vmem, vmem],
@@ -455,7 +465,7 @@
             collective_id=0, has_side_effects=True, vmem_limit_bytes=28 * 1024 * 1024
         ),
         name="reduce_and_match",
-    )(notes, keep, send, psf_kernel.T, mine)
+    )(notes, keep, send, psf_t, mine)
 
 
 def small_body(pixels, band, tile, row, weights, psf_kernel, counts_out, words_out, mine):
@@ -469,7 +479,7 @@
     keep, send = partial_sums(place, band, pixels, weights, 16 * TROWS)
     notes = jnp.concatenate([counts_out, words_out], axis=1)
     notes = jnp.broadcast_to(notes[:, :, None], notes.shape + (128,))
-    return reduce_and_match(notes, keep, send, psf_kernel, mine)
+    return reduce_and_match(notes, keep, send, psf_kernel.T, mine)
 
 
 def averaged_rows_any(pixels, band, tile, row, weights, counts_out, words_out):

time: 84.6 us -> 84.6 us (level)
  no operation moved by 1% of the time
where the time goes in v5:
time: 84.6 us; the launch traced here: 84.3 us
  Pallas kernels  75.3 us (89%)
  local copies, waits for them, and re-layouts  5.54 us (7%)
  other arithmetic  2.7 us (3%)
    pallas_call x1, Pallas kernels, reduce_and_match(): pl.pallas_call(reduce_kernel, out_shape=[jax.ShapeDtypeStruct((TROWS, psf...  67.2 us
    pallas_call x1, Pallas kernels, partial_sums(): pl.pallas_call(partial_sums_kernel, out_shape=[jax.ShapeDtypeStruct((rows...  8.15 us
    unnamed x9, local copies, waits for them, and re-layouts  4.45 us

profile of v5, /device:TPU:0, one launch (start us, length us, event | category | flops | bytes accessed | tf_op | source)
XLA Modules:
  0.0 84.3 jit_solution(2758248195130305106)
XLA Ops:
  0.7 0.7 fusion.3
  1.4 0.9 %convert_reduce_fusion.1 = s32[64]{0:T(128)S(1)} fusion(s32[64]{0:T(128)} %param.16), kind=kLoop, calls=%fused_computation.5 | loop fusion | flops 20416 | bytes 512 | tf_op jit(solution)/shard_map/reduce_sum | solution.py:516
  2.3 0.7 multiply_add_fusion
  3.0 0.1 select_reduce_fusion
  3.1 0.1 convert_reduce_fusion
  3.2 0.1 reshape.17
  3.3 0.1 reshape.18
  3.4 0.1 pad_add_fusion
  3.5 0.1 fusion.1.mine_ref
  3.5 0.1 broadcast_in_dim.18.notes_ref
  3.7 0.0 copy-start
  3.7 1.6 %copy-done = bf16[128,64,128]{2,1,0:T(8,128)(2,1)S(1)} copy-done((bf16[128,64,128]{2,1,0:T(8,128)(2,1)S(1)}, bf16[128,64,128]{2,1,0:T(8,128)(2,1)}, u32[]{:S(2)}) %copy-start) | copy-done | bytes 2097176
  5.3 0.0 copy-start.1
  5.3 0.9 %copy-done.1 = bf16[6,102,64]{1,2,0:T(8,128)(2,1)S(1)} copy-done((bf16[6,102,64]{1,2,0:T(8,128)(2,1)S(1)}, bf16[6,102,64]{1,2,0:T(8,128)(2,1)}, u32[]{:S(2)}) %copy-start.1) | copy-done | bytes 78360
  6.2 0.0 copy-start.3
  6.2 0.7 copy-done.3
  6.8 8.1 %partial_sums.1 = (bf16[128,104,128]{2,1,0:T(8,128)(2,1)S(1)}, bf16[128,104,128]{2,1,0:T(8,128)(2,1)S(1)}) custom-call(s32[128]{0:T(128)S(1)} %get-tuple-element.12.place_ref, s32[128]{0:T(128)S(1)} %copy-done.3, bf16[128,64,128]{2,1,0:T(8,128)(2,1)S(1)} %copy-done, bf16[6,64,102]{2,1,0:T(8,128)(2,1)S(1)} %bitcast.2), custom_call_target="tpu_custom_call" | custom-call | tf_op jit(solution)/shard_map/partial_sums/pallas_call | solution.py:83
  15.0 0.0 copy-start.2
  15.0 0.7 copy-done.2
  15.7 67.2 %reduce_and_match.1 = (bf16[16,102,128]{2,1,0:T(8,128)(2,1)S(1)}, bf16[64,64]{1,0:T(8,128)(2,1)S(1)}) custom-call(s32[16,24,128]{2,1,0:T(8,128)S(1)} %broadcast_in_dim.18.notes_ref, bf16[128,104,128]{2,1,0:T(8,128)(2,1)S(1)} %get-tuple-element.4.keep_hbm, bf16[128,104,128]{2,1,0:T(8,128)(2,1)S(1)} %get-tuple-element.5.send_ref, f32[25,102]{1,0:T(8,128)S(1)} %bitcast.3, ...), custom_call_target="tpu_custom_call" | custom-call | tf_op jit(solution)/shard_map/reduce_and_match/pallas_call | solution.py:435
  82.9 0.8 copy.14
  83.7 0.6 copy.16
Async XLA Ops:
  3.7 1.6 %copy-start = (bf16[128,64,128]{2,1,0:T(8,128)(2,1)S(1)}, bf16[128,64,128]{2,1,0:T(8,128)(2,1)}, u32[]{:S(2)}) copy-start(bf16[128,64,128]{2,1,0:T(8,128)(2,1)} %pixels_hbm.1) | copy-start | bytes 6291460
  5.3 0.9 %copy-start.1 = (bf16[6,102,64]{1,2,0:T(8,128)(2,1)S(1)}, bf16[6,102,64]{1,2,0:T(8,128)(2,1)}, u32[]{:S(2)}) copy-start(bf16[6,102,64]{1,2,0:T(8,128)(2,1)} %param.14) | copy-start | bytes 235012
  6.2 0.7 copy-start.3
  15.0 0.7 copy-start.2

commit v6 on v4

--- a/solution.py
+++ b/solution.py
@@ -176,7 +176,6 @@
         note(k).start()
         return 0
 
-    lax.fori_loop(1, count, send_note, 0)
 
     def cross(k):
         core_copy(1, k).wait_recv()
@@ -196,6 +195,7 @@
     core_copy(0, 0).start()
     cross(1)
     core_copy(0, 1).start()
+    lax.fori_loop(1, count, send_note, 0)
 
     def wait_note(k, total):
         note(k).wait_recv()

time: 84.6 us -> 87.7 us (1.037)
  Pallas kernels: 75.4 us -> 78.4 us
    pallas_call x1, Pallas kernels: 67.2 us -> 70.2 us  [reduce_and_match(): pl.pallas_call(reduce_kernel, out_shape=[jax.ShapeDtypeStruct((TROWS,) +...]
where the time goes in v6:
time: 87.7 us; the launch traced here: 87.4 us
  Pallas kernels  78.4 us (89%)
  local copies, waits for them, and re-layouts  5.54 us (6%)
  other arithmetic  2.7 us (3%)
    pallas_call x1, Pallas kernels, reduce_and_match(): pl.pallas_call(reduce_kernel, out_shape=[jax.ShapeDtypeStruct((TROWS,) +...  70.2 us
    pallas_call x1, Pallas kernels, partial_sums(): pl.pallas_call(partial_sums_kernel, out_shape=[jax.ShapeDtypeStruct((rows...  8.19 us
    unnamed x9, local copies, waits for them, and re-layouts  4.45 us

profile of v6, /device:TPU:0, one launch (start us, length us, event | category | flops | bytes accessed | tf_op | source)
XLA Modules:
  0.0 87.4 jit_solution(13749892265472757181)
XLA Ops:
  0.7 0.7 fusion.3
  1.4 0.9 %convert_reduce_fusion.1 = s32[64]{0:T(128)S(1)} fusion(s32[64]{0:T(128)} %param.16), kind=kLoop, calls=%fused_computation.5 | loop fusion | flops 20416 | bytes 512 | tf_op jit(solution)/shard_map/reduce_sum | solution.py:506
  2.3 0.7 multiply_add_fusion
  3.0 0.1 select_reduce_fusion
  3.1 0.1 convert_reduce_fusion
  3.2 0.1 reshape.17
  3.3 0.1 reshape.18
  3.4 0.1 pad_add_fusion
  3.5 0.1 fusion.1.mine_ref
  3.5 0.1 broadcast_in_dim.18.notes_ref
  3.7 0.0 copy-start
  3.7 1.6 %copy-done = bf16[128,64,128]{2,1,0:T(8,128)(2,1)S(1)} copy-done((bf16[128,64,128]{2,1,0:T(8,128)(2,1)S(1)}, bf16[128,64,128]{2,1,0:T(8,128)(2,1)}, u32[]{:S(2)}) %copy-start) | copy-done | bytes 2097176
  5.3 0.0 copy-start.1
  5.3 0.9 %copy-done.1 = bf16[6,102,64]{1,2,0:T(8,128)(2,1)S(1)} copy-done((bf16[6,102,64]{1,2,0:T(8,128)(2,1)S(1)}, bf16[6,102,64]{1,2,0:T(8,128)(2,1)}, u32[]{:S(2)}) %copy-start.1) | copy-done | bytes 78360
  6.2 0.0 copy-start.3
  6.2 0.7 copy-done.3
  6.8 8.2 %partial_sums.1 = (bf16[128,102,128]{2,1,0:T(8,128)(2,1)S(1)}, bf16[128,102,128]{2,1,0:T(8,128)(2,1)S(1)}) custom-call(s32[128]{0:T(128)S(1)} %get-tuple-element.12.place_ref, s32[128]{0:T(128)S(1)} %copy-done.3, bf16[128,64,128]{2,1,0:T(8,128)(2,1)S(1)} %copy-done, bf16[6,64,102]{2,1,0:T(8,128)(2,1)S(1)} %bitcast.2), custom_call_target="tpu_custom_call" | custom-call | tf_op jit(solution)/shard_map/partial_sums/pallas_call | solution.py:75
  15.0 0.0 copy-start.2
  15.0 0.7 copy-done.2
  15.7 70.2 %reduce_and_match.1 = (bf16[16,102,128]{2,1,0:T(8,128)(2,1)S(1)}, bf16[64,64]{1,0:T(8,128)(2,1)S(1)}) custom-call(s32[16,24,128]{2,1,0:T(8,128)S(1)} %broadcast_in_dim.18.notes_ref, bf16[128,102,128]{2,1,0:T(8,128)(2,1)S(1)} %get-tuple-element.4.keep_hbm, bf16[128,102,128]{2,1,0:T(8,128)(2,1)S(1)} %get-tuple-element.5.send_ref, f32[25,102]{1,0:T(8,128)S(1)} %bitcast.3, ...), custom_call_target="tpu_custom_call" | custom-call | tf_op jit(solution)/shard_map/reduce_and_match/pallas_call | solution.py:425
  85.9 0.8 copy.14
  86.8 0.6 copy.16
Async XLA Ops:
  3.7 1.6 %copy-start = (bf16[128,64,128]{2,1,0:T(8,128)(2,1)S(1)}, bf16[128,64,128]{2,1,0:T(8,128)(2,1)}, u32[]{:S(2)}) copy-start(bf16[128,64,128]{2,1,0:T(8,128)(2,1)} %pixels_hbm.1) | copy-start | bytes 6291460
  5.3 0.9 %copy-start.1 = (bf16[6,102,64]{1,2,0:T(8,128)(2,1)S(1)}, bf16[6,102,64]{1,2,0:T(8,128)(2,1)}, u32[]{:S(2)}) copy-start(bf16[6,102,64]{1,2,0:T(8,128)(2,1)} %param.14) | copy-start | bytes 235012
  6.2 0.7 copy-start.3
  15.0 0.7 copy-start.2
